TPU v7x, 32 devices: a whole 2x2x4 slice. The times are simulated.
32 devices in a mesh: row: 4 (over z), col: 8 (over y, x, core).
Axes of the slice: x: 2, y: 2, z: 4, core: 2. Of those that a mesh axis runs over, the one named last changes fastest.
Arguments:
- descriptors: bfloat16 [8192, 128], P('row'), may hold values from -6 to 6
- image_counts: int32 [32], replicated, may hold values from 64 to 256
- pair_list: int32 [256, 2], P(('row', 'col')), may hold values from 0 to 31, as said below
- warm_start: bfloat16 [8192, 8192], P('row', 'col'), may hold values from 0 to 1
- factor_init: float32 [8192, 256], P('col'), may hold values from -0.3 to 0.3
Outputs:
- assignment: bfloat16 [8192, 8192], P('row', 'col')
- dual_var: float32 [8192, 8192], P('row', 'col')
Inputs may be any that keep to these rules, and one draw needn't show every extreme that they name: `pair_list`: pairs are distinct. The 8 pairs on each device have their first image in that device's row block of 8 images, and at most 2 of them have their second image in any one column block of 4 images; in every row block some column block receives exactly 2 pairs from every device of that row group.
All inputs are finite; a program needn't handle non-finite values.
Results may differ from a plain program's by a relative error of at most 0.00055.
The roundings to bfloat16 on the way count: a program that leaves them out, or rounds other values in their place, can miss the bound.
Values may be sent and summed in bfloat16 or wider, within the bound.
A program may use at most 128 MiB of HBM per device.

v0:
```python
import jax
import jax.numpy as jnp
from jax import lax
from jax.sharding import PartitionSpec as P

KP = 256
DESC = 128
IMG_ROW = 8
ITERS = 2


EPSILON = 1e-06
SHARPNESS = 10.0
PENALTY = 2.0
RIDGE = 16.0
EXACT = lax.Precision.HIGHEST


def ridge_apply(partial_sum, gram_matrix):
    factor_low = jnp.linalg.cholesky(gram_matrix)
    half_solve = lax.linalg.triangular_solve(
        factor_low, partial_sum, left_side=False, lower=True, transpose_a=True
    )
    return lax.linalg.triangular_solve(
        factor_low, half_solve, left_side=False, lower=True, transpose_a=False
    )


def gram_share(factor_rows, axis_count, axis_place):
    share_rows = factor_rows.shape[0] // axis_count
    picked = lax.dynamic_slice_in_dim(factor_rows, axis_place * share_rows, share_rows, 0)
    local_gram = lax.dot_general(picked, picked, (((0,), (0,)), ((), ())), precision=EXACT)
    summed = lax.psum(local_gram, ("row", "col"))
    return summed + RIDGE * jnp.eye(factor_rows.shape[1], dtype=jnp.float32)


def local(descriptors, image_counts, pair_list, warm_start, factor_init):
    row_place = lax.axis_index("row")
    col_place = lax.axis_index("col")
    row_total = lax.axis_size("row")
    col_total = lax.axis_size("col")
    img_col = warm_start.shape[1] // KP
    cell_total = IMG_ROW * img_col
    wide = descriptors.astype(jnp.float32)
    unit = (
        wide * lax.rsqrt(DESC * (jnp.mean(wide * wide, axis=1, keepdims=True) + EPSILON))
    ).astype(jnp.bfloat16)
    everyone = lax.all_gather(unit, "row", axis=0, tiled=True)
    slot_iota = jnp.arange(KP, dtype=jnp.int32)
    valid_all = (slot_iota[None, :] < image_counts[:, None]).astype(jnp.float32)
    listed = lax.all_gather(pair_list, "col", axis=0, tiled=True)
    in_block = listed[:, 1] // img_col == col_place
    local_code = (listed[:, 0] - IMG_ROW * row_place) * img_col + (
        listed[:, 1] - img_col * col_place
    )
    cell_iota = jnp.arange(cell_total, dtype=jnp.int32)
    present = jnp.any((local_code[:, None] == cell_iota[None, :]) & in_block[:, None], axis=0)
    present = present.astype(jnp.float32).reshape(IMG_ROW, img_col)
    col_units = lax.dynamic_slice_in_dim(everyone, col_place * img_col * KP, img_col * KP, 0)
    scores = lax.dot_general(
        unit, col_units, (((1,), (1,)), ((), ())), preferred_element_type=jnp.float32
    )
    expo = jnp.exp(SHARPNESS * scores).reshape(IMG_ROW, KP, img_col, KP)
    valid_rows = lax.dynamic_slice_in_dim(valid_all, row_place * IMG_ROW, IMG_ROW, 0)
    valid_cols = lax.dynamic_slice_in_dim(valid_all, col_place * img_col, img_col, 0)
    rowsum = jnp.sum(expo * valid_cols[None, None, :, :], axis=3)
    colsum = jnp.sum(expo * valid_rows[:, :, None, None], axis=1)
    weights = (
        KP
        * expo
        * valid_rows[:, :, None, None]
        * valid_cols[None, None, :, :]
        / jnp.sqrt(rowsum[:, :, :, None] * colsum[:, None, :, :])
    )
    matches = (weights * present[:, None, :, None]).reshape(IMG_ROW * KP, img_col * KP)
    solution = warm_start.astype(jnp.float32)
    dual = jnp.zeros_like(solution)
    right = factor_init
    gram_right = gram_share(right, row_total, row_place)
    for sweep_index in range(ITERS):
        target = solution - dual / PENALTY
        left_terms = jnp.dot(target, right, precision=EXACT)
        left = ridge_apply(lax.psum(left_terms, "col"), gram_right)
        gram_left = gram_share(left, col_total, col_place)
        right_terms = lax.dot_general(target, left, (((0,), (0,)), ((), ())), precision=EXACT)
        right = ridge_apply(lax.psum(right_terms, "row"), gram_left)
        lowrank = lax.dot_general(left, right, (((1,), (1,)), ((), ())), precision=EXACT)
        solution = jnp.clip(lowrank + (matches + dual) / PENALTY, 0.0, 1.0)
        dual = dual + PENALTY * (solution - lowrank)
        if sweep_index + 1 < ITERS:
            gram_right = gram_share(right, row_total, row_place)
    return (solution.astype(jnp.bfloat16), dual)


def solution(mesh):
    return jax.shard_map(
        local,
        mesh=mesh,
        in_specs=(P("row", None), P(), P(("row", "col"), None), P("row", "col"), P("col", None)),
        out_specs=(P("row", "col"), P("row", "col")),
        check_vma=False,
    )
```

profile of v0, /device:TPU:0, one launch (start us, length us, event | category | flops | bytes accessed | tf_op | source)
XLA Modules:
  0.0 928.3 jit_solution(15583266431767553635)
XLA Ops:
  17.5 124.3 %all-reduce.10.cloned.1.call-done = f32[256,256]{0,1:T(8,128)} async-done(((f32[256,256]{0,1:T(8,128)}), f32[256,256]{0,1:T(8,128)}) %all-reduce.10.cloned.1.call-update) | async-done | bytes 262160 | tf_op jit(solution)/shard_map/psum | solution.py:33
  143.9 11.7 %cholesky.214 = f32[128,128]{1,0:T(8,128)S(1)} custom-call(f32[128,128]{1,0:T(8,128)S(1)} %cholesky.346), custom_call_target="Cholesky" | custom-call | tf_op jit(solution)/shard_map/jit(cholesky)/cholesky | solution.py:20
  155.6 9.8 %custom-call.27 = f32[1,128,128]{1,2,0:T(8,128)S(1)} custom-call(f32[1,128,128]{2,1,0:T(8,128)S(1)} %get-tuple-element.130), custom_call_target="InvertDiagBlocksLowerTriangular" | custom-call | tf_op jit(solution)/shard_map/jit(cholesky)/cholesky | solution.py:20
  165.9 11.7 %cholesky.231 = f32[128,128]{1,0:T(8,128)S(1)} custom-call(f32[128,128]{1,0:T(8,128)S(1)} %convolution_subtract_fusion.11), custom_call_target="Cholesky" | custom-call | tf_op jit(solution)/shard_map/jit(cholesky)/cholesky | solution.py:20
  184.1 19.7 %custom-call.28 = f32[2,128,128]{1,2,0:T(8,128)S(1)} custom-call(f32[2,128,128]{2,1,0:T(8,128)S(1)} %get-tuple-element.63), custom_call_target="InvertDiagBlocksLowerTriangular" | custom-call | tf_op jit(solution)/shard_map/triangular_solve/custom-call.0 | solution.py:21
  224.3 117.3 %all-reduce.14.cloned.1.call-done = f32[256,256]{0,1:T(8,128)} async-done(((f32[256,256]{0,1:T(8,128)}), f32[256,256]{0,1:T(8,128)}) %all-reduce.14.cloned.1.call-update) | async-done | bytes 262160 | tf_op jit(solution)/shard_map/psum | solution.py:33
  343.7 11.7 %cholesky.248 = f32[128,128]{1,0:T(8,128)S(1)} custom-call(f32[128,128]{1,0:T(8,128)S(1)} %cholesky.349), custom_call_target="Cholesky" | custom-call | tf_op jit(solution)/shard_map/jit(cholesky)/cholesky | solution.py:20
  355.4 9.8 %custom-call.30 = f32[1,128,128]{1,2,0:T(8,128)S(1)} custom-call(f32[1,128,128]{2,1,0:T(8,128)S(1)} %get-tuple-element.126), custom_call_target="InvertDiagBlocksLowerTriangular" | custom-call | tf_op jit(solution)/shard_map/jit(cholesky)/cholesky | solution.py:20
  365.7 11.7 %cholesky.265 = f32[128,128]{1,0:T(8,128)S(1)} custom-call(f32[128,128]{1,0:T(8,128)S(1)} %convolution_subtract_fusion.10), custom_call_target="Cholesky" | custom-call | tf_op jit(solution)/shard_map/jit(cholesky)/cholesky | solution.py:20
  384.8 19.7 %custom-call.31 = f32[2,128,128]{1,2,0:T(8,128)S(1)} custom-call(f32[2,128,128]{2,1,0:T(8,128)S(1)} %get-tuple-element.65), custom_call_target="InvertDiagBlocksLowerTriangular" | custom-call | tf_op jit(solution)/shard_map/triangular_solve/custom-call.5 | solution.py:21
  438.7 96.9 %all-reduce.18.cloned.1.call-done = f32[256,256]{0,1:T(8,128)} async-done(((f32[256,256]{0,1:T(8,128)}), f32[256,256]{0,1:T(8,128)}) %all-reduce.18.cloned.1.call-update) | async-done | bytes 262160 | tf_op jit(solution)/shard_map/psum | solution.py:33
  537.7 11.7 %cholesky.282 = f32[128,128]{1,0:T(8,128)S(1)} custom-call(f32[128,128]{1,0:T(8,128)S(1)} %cholesky.352), custom_call_target="Cholesky" | custom-call | tf_op jit(solution)/shard_map/jit(cholesky)/cholesky | solution.py:20
  559.7 11.7 %cholesky.299 = f32[128,128]{1,0:T(8,128)S(1)} custom-call(f32[128,128]{1,0:T(8,128)S(1)} %convolution_subtract_fusion.9), custom_call_target="Cholesky" | custom-call | tf_op jit(solution)/shard_map/jit(cholesky)/cholesky | solution.py:20
  571.5 11.4 %all-gather.3.cloned.1.call-done = bf16[8192,128]{1,0:T(8,128)(2,1)} async-done(((bf16[2048,128]{1,0:T(8,128)(2,1)}), bf16[8192,128]{1,0:T(8,128)(2,1)}) %all-gather.3.cloned.1.call-update) | async-done | bytes 2097168 | tf_op jit(solution)/shard_map/all_gather | solution.py:48
  588.5 10.5 %reshape.73 = f32[8,256,4,256]{3,2,1,0:T(4,128)} reshape(f32[2048,1024]{1,0:T(8,128)} %multiply_exponential_fusion) | data formatting | bytes 16777216 | tf_op jit(solution)/shard_map/reshape | solution.py:63
  646.7 19.7 %custom-call.34 = f32[2,128,128]{1,2,0:T(8,128)S(1)} custom-call(f32[2,128,128]{2,1,0:T(8,128)S(1)} %get-tuple-element.67), custom_call_target="InvertDiagBlocksLowerTriangular" | custom-call | tf_op jit(solution)/shard_map/triangular_solve/custom-call.0 | solution.py:21
  666.4 34.3 %all-reduce.20.cloned.1.call-done = f32[2048,256]{1,0:T(8,128)} async-done(((f32[2048,256]{1,0:T(8,128)}), f32[2048,256]{1,0:T(8,128)}) %all-reduce.20.cloned.1.call-update) | async-done | bytes 2097168 | tf_op jit(solution)/shard_map/psum | solution.py:83
  711.5 17.6 %fusion.8 = f32[1024,256]{1,0:T(8,128)} fusion(f32[2048,128]{0,1:T(8,128)S(1)} %bitcast.208, f32[2048,128]{0,1:T(8,128)S(1)} %fusion.71, f32[2048,1024]{1,0:T(8,128)} %fusion.11, f32[2048,1024]{1,0:T(8,128)} %copy-done.3), kind=kOutput, calls=%fused_computation.32 | convolution fusion | flops 6453460992 | bytes 19922944 | tf_op jit(solution)/shard_map/dot_general | solution.py:85
  729.1 106.7 %all-reduce.22.cloned.1.call-done = f32[256,256]{0,1:T(8,128)} async-done(((f32[256,256]{0,1:T(8,128)}), f32[256,256]{0,1:T(8,128)}) %all-reduce.22.cloned.1.call-update) | async-done | bytes 262160 | tf_op jit(solution)/shard_map/psum | solution.py:33
  837.9 11.7 %cholesky.316 = f32[128,128]{1,0:T(8,128)S(1)} custom-call(f32[128,128]{1,0:T(8,128)S(1)} %cholesky.355), custom_call_target="Cholesky" | custom-call | tf_op jit(solution)/shard_map/jit(cholesky)/cholesky | solution.py:20
  849.7 9.8 %custom-call.36 = f32[1,128,128]{1,2,0:T(8,128)S(1)} custom-call(f32[1,128,128]{2,1,0:T(8,128)S(1)} %get-tuple-element.118), custom_call_target="InvertDiagBlocksLowerTriangular" | custom-call | tf_op jit(solution)/shard_map/jit(cholesky)/cholesky | solution.py:20
  860.0 11.7 %cholesky.333 = f32[128,128]{1,0:T(8,128)S(1)} custom-call(f32[128,128]{1,0:T(8,128)S(1)} %convolution_subtract_fusion.8), custom_call_target="Cholesky" | custom-call | tf_op jit(solution)/shard_map/jit(cholesky)/cholesky | solution.py:20
  878.6 19.9 %custom-call.37 = f32[2,128,128]{1,2,0:T(8,128)S(1)} custom-call(f32[2,128,128]{2,1,0:T(8,128)S(1)} %get-tuple-element.69), custom_call_target="InvertDiagBlocksLowerTriangular" | custom-call | tf_op jit(solution)/shard_map/triangular_solve/custom-call.5 | solution.py:21
  904.8 16.5 %multiply_add_fusion = (f32[2048,1024]{1,0:T(8,128)}, bf16[2048,1024]{1,0:T(8,128)(2,1)}) fusion(f32[2048,1024]{1,0:T(8,128)} %fusion.11, f32[2048,1024]{1,0:T(8,128)} %copy-done.3, f32[1024,128]{0,1:T(8,128)S(1)} %bitcast.216, f32[1024,128]{0,1:T(8,128)S(1)} %fusion.74, f32[2048,128]{0,1:T(8,128)S(1)} %bitcast.209, f32[2048,128]{0,1:T(8,128)S(1)} %fusion.71), kind=kOutput, calls=%fused_computation.9 | convolution fusion | flops 6470500352 | bytes 32505856 | tf_op jit(solution)/shard_map/dot_general | solution.py:87
  (178 shorter events, 186.6 us)
Async XLA Ops:
  7.2 1.2 copy-start
  7.2 9.9 %copy-start.4 = (bf16[2048,128]{1,0:T(8,128)(2,1)S(1)}, bf16[2048,128]{1,0:T(8,128)(2,1)}, u32[]{:S(2)}) copy-start(bf16[2048,128]{1,0:T(8,128)(2,1)} %param.14) | copy-start | bytes 1572868
  7.2 134.5 %all-reduce.10.cloned.1.call-start = ((), (), s32[]{:S(2)}) async-start(), calls=%async_computation | async-start | bytes 524288 | tf_op jit(solution)/shard_map/psum | solution.py:33
  9.7 196.9 %all-reduce.12.cloned.1.call-start = ((), (), s32[]{:S(2)}) async-start(), calls=%async_computation.1 | async-start | bytes 4194304 | tf_op jit(solution)/shard_map/psum | solution.py:83
  16.8 324.7 %all-reduce.14.cloned.1.call-start = ((), (), s32[]{:S(2)}) async-start(), calls=%async_computation.2 | async-start | bytes 524288 | tf_op jit(solution)/shard_map/psum | solution.py:33
  217.4 187.1 %all-reduce.16.cloned.1.call-start = ((), (), s32[]{:S(2)}) async-start(), calls=%async_computation.3 | async-start | bytes 2097152 | tf_op jit(solution)/shard_map/psum | solution.py:86
  224.0 189.7 %copy-start.5 = (s32[8,2]{0,1:T(2,128)S(1)}, s32[8,2]{0,1:T(2,128)}, u32[]{:S(2)}) copy-start(s32[8,2]{0,1:T(2,128)} %param.16) | copy-start | bytes 196
  224.0 311.5 %all-reduce.18.cloned.1.call-start = ((), (), s32[]{:S(2)}) async-start(), calls=%async_computation.4 | async-start | bytes 524288 | tf_op jit(solution)/shard_map/psum | solution.py:33
  411.4 171.5 %all-gather.3.cloned.1.call-start = ((), (), s32[]{:S(2)}) async-start(), calls=%async_computation.5 | async-start | bytes 2621440 | tf_op jit(solution)/shard_map/all_gather | solution.py:48
  413.6 287.0 %all-reduce.20.cloned.1.call-start = ((), (), s32[]{:S(2)}) async-start(), calls=%async_computation.6 | async-start | bytes 4194304 | tf_op jit(solution)/shard_map/psum | solution.py:83
  424.0 5.3 copy-start.6
  599.0 6.2 copy-start.2
  609.6 21.2 %slice-start = ((s8[8388608]{0:T(1024)(128)(4,1)}), s8[4194304]{0:T(1024)(128)(4,1)S(1)}, s32[]{:S(2)}) async-start(s8[8388608]{0:T(1024)(128)(4,1)} %bitcast.201), calls=%async_computation.9 | async-start | bytes 8388608
  618.5 12.4 %slice-start.1 = ((s8[8388608]{0:T(1024)(128)(4,1)}), s8[4194304]{0:T(1024)(128)(4,1)S(1)}, s32[]{:S(2)}) async-start(s8[8388608]{0:T(1024)(128)(4,1)} %bitcast.201), calls=%async_computation.10 | async-start | bytes 8388608
  627.6 3.2 copy-start.3
  640.0 195.9 %all-reduce.22.cloned.1.call-start = ((), (), s32[]{:S(2)}) async-start(), calls=%async_computation.7 | async-start | bytes 524288 | tf_op jit(solution)/shard_map/psum | solution.py:33
  711.4 187.2 %all-reduce.24.cloned.1.call-start = ((), (), s32[]{:S(2)}) async-start(), calls=%async_computation.8 | async-start | bytes 2097152 | tf_op jit(solution)/shard_map/psum | solution.py:86
  904.8 16.5 %copy-start.1 = (f32[1024,256]{1,0:T(8,128)S(1)}, f32[1024,256]{1,0:T(8,128)}, u32[]{:S(2)}) copy-start(f32[1024,256]{1,0:T(8,128)} %param.18) | copy-start | bytes 3145732
Sparse Core Ops, SparseCore 0:
  14.1 127.5 all-reduce.9
  145.5 61.0 all-reduce.11
  217.5 124.0 all-reduce.13
  344.3 51.0 all-reduce.15
  411.5 123.9 all-reduce.17
  537.6 45.2 all-gather.2
  640.1 60.5 all-reduce.19
  711.6 124.2 all-reduce.21
  838.9 51.2 all-reduce.23
where the time goes:
time: 933 us; the launch traced here: 928 us
  waiting for transfers between devices  494 us (53%)
  other arithmetic  247 us (26%)
  matrix products  109 us (12%)
  local copies, waits for them, and re-layouts  47.1 us (5%)
  between operations  20.1 us (2%)
    psum x4, waiting for transfers between devices, gram_share(): summed = lax.psum(local_gram, ('row', 'col'))  445 us
    another operation x27, other arithmetic, ridge_apply(): factor_low = jnp.linalg.cholesky(gram_matrix)  138 us
    another operation x9, other arithmetic, ridge_apply(): lax.linalg.triangular_solve(factor_low, partial_sum, left_side=False, low...  79.1 us
    psum x2, waiting for transfers between devices, local(): left = ridge_apply(lax.psum(left_terms, 'col'), gram_right)  37.1 us
    dot_general x2, matrix products, local(): lax.dot_general(left, right, (((1,), (1,)), ((), ())), precision=EXACT)  25.7 us
    dot_general x2, matrix products, local(): lax.dot_general(target, left, (((0,), (0,)), ((), ())), precision=EXACT)  24.2 us
    another operation x12, matrix products, ridge_apply(): lax.linalg.triangular_solve(factor_low, partial_sum, left_side=False, low...  21.1 us
    unnamed x24, local copies, waits for them, and re-layouts  18.7 us
  transfers between devices with their start and end apart: 9, of which 7 were waited for; matrix products, arithmetic and copies ran while one was open for 32% of the time, Pallas kernels for 0%

commit v1 on v0

v1 whole, which is shorter than its diff:
```python
import functools

import jax
import jax.numpy as jnp
from jax import lax
from jax.experimental import pallas as pl
from jax.experimental.pallas import tpu as pltpu
from jax.sharding import PartitionSpec as P

KP = 256

EPSILON = 1e-06
SHARPNESS = 10.0
RIDGE = 16.0
EXACT = lax.Precision.HIGHEST
F32 = jnp.float32
BF16 = jnp.bfloat16
PARAMS = pltpu.CompilerParams(vmem_limit_bytes=48 * 1024 * 1024)
SETTLED = 2e-4


def halves(x):
    high = x.astype(BF16)
    return high, (x - high.astype(F32)).astype(BF16)


def dot32(a, b):
    return jnp.dot(a, b, preferred_element_type=F32)


def exact(a, b):
    return jnp.dot(a, b, precision=EXACT, preferred_element_type=F32)


def eye(n):
    return (
        lax.broadcasted_iota(jnp.int32, (n, n), 0) == lax.broadcasted_iota(jnp.int32, (n, n), 1)
    ).astype(F32)


def invert(matrix_ref, inverse_ref):
    n = matrix_ref.shape[0]
    top = jnp.max(jnp.sum(jnp.abs(matrix_ref[...]), axis=1, keepdims=True))
    inverse_ref[...] = (2.0 / (RIDGE + top)) * eye(n)

    def step(spread):
        scale = 2.0 / (2.0 - spread * spread)
        rest = (2.0 * scale) * eye(n) - scale * exact(matrix_ref[...], inverse_ref[...])
        inverse_ref[...] = exact(inverse_ref[...], rest)
        return spread * spread / (2.0 - spread * spread)

    spread = lax.while_loop(lambda s: s > SETTLED, step, (top - RIDGE) / (top + RIDGE))
    step(spread)


def inverse_body(gram_ref, out_ref, matrix_ref):
    matrix_ref[...] = gram_ref[...] + RIDGE * eye(gram_ref.shape[0])
    invert(matrix_ref, out_ref)


def ridge_inverse(gram):
    return pl.pallas_call(
        inverse_body,
        out_shape=jax.ShapeDtypeStruct(gram.shape, F32),
        scratch_shapes=[pltpu.VMEM(gram.shape, F32)],
        compiler_params=PARAMS,
        name="ridge_inverse",
        cost_estimate=pl.CostEstimate(flops=200 * gram.shape[0] ** 3, bytes_accessed=8 * gram.size, transcendentals=0),
    )(gram)


def second_body(gram_right_ref, gram_left_ref, out_ref, matrix_ref, inverse_ref, filter_ref):
    n = out_ref.shape[0]
    matrix_ref[...] = gram_right_ref[...] + RIDGE * eye(n)
    invert(matrix_ref, inverse_ref)
    filter_ref[...] = eye(n) - RIDGE * inverse_ref[...]
    out_ref[...] = exact(filter_ref[...], gram_left_ref[...])
    matrix_ref[...] = exact(out_ref[...], filter_ref[...]) + RIDGE * eye(n)
    invert(matrix_ref, inverse_ref)
    out_ref[...] = exact(exact(filter_ref[...], inverse_ref[...]), out_ref[...])


def second_mix(gram_right, gram_left):
    n = gram_right.shape[0]
    return pl.pallas_call(
        second_body,
        out_shape=jax.ShapeDtypeStruct((n, n), F32),
        scratch_shapes=[pltpu.VMEM((n, n), F32)] * 3,
        compiler_params=PARAMS,
        name="second_mix",
        cost_estimate=pl.CostEstimate(flops=400 * n**3, bytes_accessed=12 * n * n, transcendentals=0),
    )(gram_right, gram_left)


def left_sum_body(warm_ref, right_ref, out_ref, high_ref, low_ref):
    @pl.when(pl.program_id(0) == 0)
    def _():
        high_ref[...], low_ref[...] = halves(right_ref[...])

    out_ref[...] = dot32(warm_ref[...], high_ref[...]) + dot32(warm_ref[...], low_ref[...])


def left_sum(warm, right):
    rows, cols = warm.shape
    rank = right.shape[1]
    return pl.pallas_call(
        left_sum_body,
        grid=(rows // KP,),
        in_specs=[
            pl.BlockSpec((KP, cols), lambda i: (i, 0)),
            pl.BlockSpec((cols, rank), lambda i: (0, 0)),
        ],
        out_specs=pl.BlockSpec((KP, rank), lambda i: (i, 0)),
        out_shape=jax.ShapeDtypeStruct((rows, rank), F32),
        scratch_shapes=[pltpu.VMEM((cols, rank), BF16)] * 2,
        compiler_params=PARAMS,
        name="left_sum",
        cost_estimate=pl.CostEstimate(flops=4 * rows * cols * rank, bytes_accessed=2 * rows * cols, transcendentals=0),
    )(warm, right)


def right_sum_body(left_ref, warm_ref, out_ref, turned_ref):
    rank = out_ref.shape[0]

    @pl.when(pl.program_id(0) == 0)
    def _():
        turned_ref[...] = left_ref[...].T

    out_ref[...] = dot32(turned_ref[:rank, :], warm_ref[...]) + dot32(turned_ref[rank:, :], warm_ref[...])


def right_sum(left_pair, warm):
    rows, cols = warm.shape
    rank = left_pair.shape[1] // 2
    return pl.pallas_call(
        right_sum_body,
        grid=(cols // KP,),
        in_specs=[
            pl.BlockSpec((rows, 2 * rank), lambda i: (0, 0)),
            pl.BlockSpec((rows, KP), lambda i: (0, i)),
        ],
        out_specs=pl.BlockSpec((rank, KP), lambda i: (0, i)),
        out_shape=jax.ShapeDtypeStruct((rank, cols), F32),
        scratch_shapes=[pltpu.VMEM((2 * rank, rows), BF16)],
        compiler_params=PARAMS,
        name="right_sum",
        cost_estimate=pl.CostEstimate(flops=4 * rows * cols * rank, bytes_accessed=2 * rows * cols, transcendentals=0),
    )(left_pair, warm)


def left_apply_body(terms_ref, inverse_ref, pair_ref, gram_ref):
    rank = terms_ref.shape[1]
    left = exact(terms_ref[...], inverse_ref[...])
    high, low = halves(left)
    pair_ref[:, :rank] = high
    pair_ref[:, rank:] = low
    gram_ref[...] = exact(left.T, left)


def left_apply(terms, inverse):
    rows, rank = terms.shape
    return pl.pallas_call(
        left_apply_body,
        out_shape=(jax.ShapeDtypeStruct((rows, 2 * rank), BF16), jax.ShapeDtypeStruct((rank, rank), F32)),
        compiler_params=PARAMS,
        name="left_apply",
    )(terms, inverse)


def right_apply_body(terms_ref, inverse_ref, pair_ref, gram_ref):
    rank = terms_ref.shape[0]
    right = exact(inverse_ref[...], terms_ref[...])
    high, low = halves(right)
    pair_ref[:rank, :] = high
    pair_ref[rank:, :] = low
    gram_ref[...] = exact(right, right.T)


def right_apply(terms, inverse):
    rank, cols = terms.shape
    return pl.pallas_call(
        right_apply_body,
        out_shape=(jax.ShapeDtypeStruct((2 * rank, cols), BF16), jax.ShapeDtypeStruct((rank, rank), F32)),
        compiler_params=PARAMS,
        name="right_apply",
    )(terms, inverse)


def finish_body(
    img_col,
    present_ref, row_count_ref, col_count_ref,
    row_unit_ref, col_unit_ref, left_ref, right_ref, mix_ref,
    assign_ref, dual_ref,
    second_ref, match_ref,
):
    rank = mix_ref.shape[0]
    step = pl.program_id(0)

    @pl.when(step == 0)
    def _():
        mix_high, mix_low = halves(mix_ref[...])
        high, low = right_ref[:rank, :], right_ref[rank:, :]
        mixed = dot32(mix_high, high) + dot32(mix_low, high) + dot32(mix_high, low)
        second_ref[:rank, :], second_ref[rank:, :] = halves(mixed)

    row_valid = lax.broadcasted_iota(jnp.int32, (KP, 1), 0) < row_count_ref[step]
    for image in range(img_col):
        cell = slice(image * KP, (image + 1) * KP)
        listed = present_ref[step * img_col + image] > 0

        @pl.when(listed)
        def _():
            scores = lax.dot_general(
                row_unit_ref[...], col_unit_ref[cell, :], (((1,), (1,)), ((), ())), preferred_element_type=F32
            )
            expo = jnp.exp(SHARPNESS * scores)
            col_valid = lax.broadcasted_iota(jnp.int32, (1, KP), 1) < col_count_ref[image]
            by_col = jnp.where(col_valid, expo, 0.0)
            by_row = jnp.where(row_valid, expo, 0.0)
            rowsum = jnp.sum(by_col, axis=1, keepdims=True)
            colsum = jnp.sum(by_row, axis=0, keepdims=True)
            both = jnp.where(row_valid, by_col, 0.0)
            match_ref[:, cell] = both * ((0.5 * KP) * lax.rsqrt(rowsum)) * lax.rsqrt(colsum)

        @pl.when(jnp.logical_not(listed))
        def _():
            match_ref[:, cell] = jnp.zeros((KP, KP), F32)

        left_high, left_low = left_ref[:, :rank], left_ref[:, rank:]

        def product(ref):
            high = ref[:rank, cell]
            return dot32(left_high, high) + dot32(left_high, ref[rank:, cell]) + dot32(left_low, high)

        half_match = match_ref[:, cell]
        lowrank = product(right_ref)
        half_dual = jnp.clip(lowrank + half_match, 0.0, 1.0) - lowrank
        lowrank = product(second_ref)
        solution = jnp.clip(lowrank + (half_match + half_dual), 0.0, 1.0)
        dual_ref[:, cell] = 2.0 * (half_dual + (solution - lowrank))
        assign_ref[:, cell] = solution.astype(BF16)


def finish(present, row_count, col_count, row_unit, col_unit, left_pair, right_pair, mix):
    rows, rank = left_pair.shape[0], mix.shape[0]
    cols = right_pair.shape[1]
    img_col = cols // KP
    smem = pl.BlockSpec(memory_space=pltpu.SMEM)
    return pl.pallas_call(
        functools.partial(finish_body, img_col),
        grid=(rows // KP,),
        in_specs=[
            smem, smem, smem,
            pl.BlockSpec((KP, row_unit.shape[1]), lambda i: (i, 0)),
            pl.BlockSpec(col_unit.shape, lambda i: (0, 0)),
            pl.BlockSpec((KP, 2 * rank), lambda i: (i, 0)),
            pl.BlockSpec((2 * rank, cols), lambda i: (0, 0)),
            pl.BlockSpec((rank, rank), lambda i: (0, 0)),
        ],
        out_specs=(pl.BlockSpec((KP, cols), lambda i: (i, 0)), pl.BlockSpec((KP, cols), lambda i: (i, 0))),
        out_shape=(jax.ShapeDtypeStruct((rows, cols), BF16), jax.ShapeDtypeStruct((rows, cols), F32)),
        scratch_shapes=[pltpu.VMEM((2 * rank, cols), BF16), pltpu.VMEM((KP, cols), F32)],
        compiler_params=PARAMS,
        name="finish",
        cost_estimate=pl.CostEstimate(flops=12 * rows * cols * rank, bytes_accessed=6 * rows * cols, transcendentals=rows * cols),
    )(present, row_count, col_count, row_unit, col_unit, left_pair, right_pair, mix)


def local(descriptors, image_counts, pair_list, warm_start, factor_init):
    row_place = lax.axis_index("row")
    col_place = lax.axis_index("col")
    rows, cols = warm_start.shape
    img_row, img_col = rows // KP, cols // KP

    left_terms = left_sum(warm_start, factor_init)
    gram_right = lax.psum(lax.dot_general(factor_init, factor_init, (((0,), (0,)), ((), ())), precision=EXACT), "col")
    left_terms = lax.psum_scatter(left_terms, "col", scatter_dimension=0, tiled=True)

    wide = descriptors.astype(F32)
    unit = (
        wide * lax.rsqrt(descriptors.shape[1] * (jnp.mean(wide * wide, axis=1, keepdims=True) + EPSILON))
    ).astype(BF16)
    everyone = lax.all_gather(unit, "row", axis=0, tiled=True)
    col_unit = lax.dynamic_slice_in_dim(everyone, col_place * cols, cols, 0)
    listed = lax.all_gather(pair_list, "col", axis=0, tiled=True)
    in_block = listed[:, 1] // img_col == col_place
    local_code = (listed[:, 0] - img_row * row_place) * img_col + (listed[:, 1] - img_col * col_place)
    cell_iota = jnp.arange(img_row * img_col, dtype=jnp.int32)
    present = jnp.any((local_code[:, None] == cell_iota[None, :]) & in_block[:, None], axis=0).astype(jnp.int32)
    row_count = lax.dynamic_slice_in_dim(image_counts, row_place * img_row, img_row, 0)
    col_count = lax.dynamic_slice_in_dim(image_counts, col_place * img_col, img_col, 0)

    left_pair, gram_left = left_apply(left_terms, ridge_inverse(gram_right))
    gram_left = lax.psum(gram_left, ("row", "col"))
    left_pair = lax.all_gather(left_pair, "col", axis=0, tiled=True)
    right_terms = lax.psum_scatter(right_sum(left_pair, warm_start), "row", scatter_dimension=1, tiled=True)
    right_pair, gram_right = right_apply(right_terms, ridge_inverse(gram_left))
    gram_right = lax.psum(gram_right, ("row", "col"))
    right_pair = lax.all_gather(right_pair, "row", axis=1, tiled=True)
    mix = second_mix(gram_right, gram_left)
    return finish(present, row_count, col_count, unit, col_unit, left_pair, right_pair, mix)


def solution(mesh):
    return jax.shard_map(
        local,
        mesh=mesh,
        in_specs=(P("row", None), P(), P(("row", "col"), None), P("row", "col"), P("col", None)),
        out_specs=(P("row", "col"), P("row", "col")),
        check_vma=False,
    )
```

time: 933 us -> 540 us (0.58)
  other arithmetic: 247 us -> 1.63 us
  matrix products: 109 us -> 4.14 us
  Pallas kernels: 0 us -> 75.1 us
  waiting for transfers between devices: 494 us -> 424 us
  local copies, waits for them, and re-layouts: 47.1 us -> 8.79 us
    another operation x36 -> x0, other arithmetic: 217 us -> none  [the longest x27 138 us: ridge_apply(): factor_low = jnp.linalg.cholesky(gram_matrix)]
    psum x8 -> x3, waiting for transfers between devices: 482 us -> 299 us  [the longest x1 129 us: local(): gram_right = lax.psum(gram_right, ('row', 'col'))]
    pallas_call x0 -> x8, Pallas kernels: none -> 75.1 us  [the longest x1 21.2 us: second_mix(): pl.pallas_call(second_body, out_shape=jax.ShapeDtypeStruct((n, n), F32),...]
    dot_general x11 -> x1, matrix products: 76.3 us -> 4.14 us  [local(): lax.dot_general(factor_init, factor_init, (((0,), (0,)), ((), ())), preci...]
    reduce_scatter x0 -> x2, waiting for transfers between devices: none -> 53.7 us  [the longest x1 36 us: local(): lax.psum_scatter(left_terms, 'col', scatter_dimension=0, tiled=True)]
    all_gather x0 -> x2, waiting for transfers between devices: none -> 36.7 us  [the longest x1 27.4 us: local(): left_pair = lax.all_gather(left_pair, 'col', axis=0, tiled=True)]
    another operation x32 -> x0, matrix products: 32.8 us -> none  [the longest x12 21.1 us: ridge_apply(): lax.linalg.triangular_solve(factor_low, partial_sum, left_side=False, low...]
    all_gather x1, waiting for transfers between devices: 11.4 us -> 34 us  [local(): everyone = lax.all_gather(unit, 'row', axis=0, tiled=True)]
  transfers between devices with their start and end apart: 9 -> 8, of which waited for: 7 -> 8; matrix products, arithmetic and copies ran while one was open for 32% -> 1% of each run, Pallas kernels for 0% -> 10%
where the time goes in v1:
time: 540 us; the launch traced here: 537 us
  waiting for transfers between devices  424 us (79%)
  Pallas kernels  75.1 us (14%)
  between operations  14.3 us (3%)
  blocking collectives  8.85 us (2%)
  local copies, waits for them, and re-layouts  8.79 us (2%)
    psum x1, waiting for transfers between devices, local(): gram_right = lax.psum(gram_right, ('row', 'col'))  129 us
    psum x1, waiting for transfers between devices, local(): gram_left = lax.psum(gram_left, ('row', 'col'))  121 us
    psum x1, waiting for transfers between devices, local(): lax.psum(lax.dot_general(factor_init, factor_init, (((0,), (0,)), ((), ()...  48.6 us
    reduce_scatter x1, waiting for transfers between devices, local(): lax.psum_scatter(left_terms, 'col', scatter_dimension=0, tiled=True)  36 us
    all_gather x1, waiting for transfers between devices, local(): everyone = lax.all_gather(unit, 'row', axis=0, tiled=True)  34 us
    all_gather x1, waiting for transfers between devices, local(): left_pair = lax.all_gather(left_pair, 'col', axis=0, tiled=True)  27.4 us
    pallas_call x1, Pallas kernels, second_mix(): pl.pallas_call(second_body, out_shape=jax.ShapeDtypeStruct((n, n), F32),...  21.2 us
    pallas_call x2, Pallas kernels, ridge_inverse(): pl.pallas_call(inverse_body, out_shape=jax.ShapeDtypeStruct(gram.shape, F...  18.2 us
  transfers between devices with their start and end apart: 8, of which 8 were waited for; matrix products, arithmetic and copies ran while one was open for 1% of the time, Pallas kernels for 10%

profile of v1, /device:TPU:0, one launch (start us, length us, event | category | flops | bytes accessed | tf_op | source)
XLA Modules:
  0.0 537.5 jit_solution(6819971317897827490)
XLA Ops:
  7.2 4.1 fusion.4
  11.4 7.8 %left_sum.1 = f32[2048,256]{1,0:T(8,128)} custom-call(bf16[2048,1024]{1,0:T(8,128)(2,1)} %warm_ref.3, f32[1024,256]{1,0:T(8,128)S(1)} %copy-done), custom_call_target="tpu_custom_call" | custom-call | flops 2147483648 | bytes 4194304 | tf_op jit(solution)/shard_map/left_sum/pallas_call | solution.py:106
  19.3 48.6 %all-reduce.4.cloned.1.call-done.gram_ref = f32[256,256]{1,0:T(8,128)} async-done(((f32[256,256]{1,0:T(8,128)}), f32[256,256]{1,0:T(8,128)}) %all-reduce.4.cloned.1.call-update) | async-done | bytes 262160 | tf_op jit(solution)/shard_map/psum | solution.py:276
  68.8 8.0 %ridge_inverse.2.inverse_ref = f32[256,256]{1,0:T(8,128)S(1)} custom-call(f32[256,256]{1,0:T(8,128)S(1)} %copy-done.10), custom_call_target="tpu_custom_call" | custom-call | flops 3355443200 | bytes 524288 | tf_op jit(solution)/shard_map/ridge_inverse/pallas_call | solution.py:62
  76.8 36.0 %reduce-scatter.3.cloned.1.call-done.terms_ref = f32[256,256]{1,0:T(8,128)} async-done(((f32[2048,256]{1,0:T(8,128)}), f32[256,256]{1,0:T(8,128)}) %reduce-scatter.3.cloned.1.call-update) | async-done | bytes 262160 | tf_op jit(solution)/shard_map/reduce_scatter | solution.py:277
  112.8 0.9 copy-done.3
  113.8 1.8 left_apply.1
  116.2 27.4 %all-gather.7.cloned.1.call-done.left_ref = bf16[2048,512]{1,0:T(8,128)(2,1)} async-done(((bf16[256,512]{1,0:T(8,128)(2,1)}), bf16[2048,512]{1,0:T(8,128)(2,1)}) %all-gather.7.cloned.1.call-update) | async-done | bytes 2097168 | tf_op jit(solution)/shard_map/all_gather | solution.py:295
  143.7 1.6 copy-done.4
  145.2 6.2 %right_sum.1 = f32[256,1024]{1,0:T(8,128)} custom-call(bf16[2048,512]{1,0:T(8,128)(2,1)S(1)} %copy-done.4, bf16[2048,1024]{1,0:T(8,128)(2,1)} %warm_ref.3), custom_call_target="tpu_custom_call" | custom-call | flops 2147483648 | bytes 4194304 | tf_op jit(solution)/shard_map/right_sum/pallas_call | solution.py:135
  151.9 1.1 fusion.1.row_unit_ref
  153.1 120.9 %all-reduce.6.cloned.1.call-done.gram_ref.gram_left_ref = f32[256,256]{1,0:T(8,128)} async-done(((f32[256,256]{1,0:T(8,128)}), f32[256,256]{1,0:T(8,128)}) %all-reduce.6.cloned.1.call-update) | async-done | bytes 262160 | tf_op jit(solution)/shard_map/psum | solution.py:294
  275.0 10.2 %ridge_inverse.3.inverse_ref = f32[256,256]{1,0:T(8,128)S(1)} custom-call(f32[256,256]{1,0:T(8,128)S(1)} %copy-done.7), custom_call_target="tpu_custom_call" | custom-call | flops 3355443200 | bytes 524288 | tf_op jit(solution)/shard_map/ridge_inverse/pallas_call | solution.py:62
  285.2 17.8 %reduce-scatter.5.cloned.1.call-done.terms_ref = f32[256,256]{1,0:T(8,128)} async-done(((f32[256,1024]{1,0:T(8,128)}), f32[256,256]{1,0:T(8,128)}) %reduce-scatter.5.cloned.1.call-update) | async-done | bytes 262160 | tf_op jit(solution)/shard_map/reduce_scatter | solution.py:296
  303.9 1.8 right_apply.1
  306.6 8.8 %all-gather = s32[8,8,2]{1,2,0:T(2,128)S(1)} all-gather(s32[1,8,2]{1,2,0:T(2,128)S(1)} %bitcast.9), channel_id=1, replica_groups=mesh['row'=4,'col'=8] {'col'}, dimensions={0}, use_global_device_ids=true | all-gather | bytes 576 | tf_op jit(solution)/shard_map/all_gather | solution.py:285
  315.7 34.0 %all-gather.5.cloned.1.call-done = bf16[8192,128]{1,0:T(8,128)(2,1)} async-done(((bf16[2048,128]{1,0:T(8,128)(2,1)}), bf16[8192,128]{1,0:T(8,128)(2,1)}) %all-gather.5.cloned.1.call-update) | async-done | bytes 2097168 | tf_op jit(solution)/shard_map/all_gather | solution.py:283
  349.7 1.0 constant_dynamic-slice_fusion.col_unit_ref
  350.7 129.1 %all-reduce.8.cloned.1.call-done.gram_right_ref = f32[256,256]{1,0:T(8,128)} async-done(((f32[256,256]{1,0:T(8,128)}), f32[256,256]{1,0:T(8,128)}) %all-reduce.8.cloned.1.call-update) | async-done | bytes 262160 | tf_op jit(solution)/shard_map/psum | solution.py:298
  479.8 0.9 copy-done.9
  480.8 21.2 %second_mix.1.mix_ref = f32[256,256]{1,0:T(8,128)S(1)} custom-call(f32[256,256]{1,0:T(8,128)S(1)} %copy-done.9, f32[256,256]{1,0:T(8,128)S(1)} %copy-done.8), custom_call_target="tpu_custom_call" | custom-call | flops 6710886400 | bytes 786432 | tf_op jit(solution)/shard_map/second_mix/pallas_call | solution.py:85
  502.0 9.3 %all-gather.9.cloned.1.call-done.right_ref = bf16[512,1024]{1,0:T(8,128)(2,1)} async-done(((bf16[512,256]{1,0:T(8,128)(2,1)}), bf16[512,1024]{1,0:T(8,128)(2,1)}) %all-gather.9.cloned.1.call-update) | async-done | bytes 1048592 | tf_op jit(solution)/shard_map/all_gather | solution.py:299
  511.3 1.2 copy-done.6
  512.6 18.1 %finish.1 = (bf16[2048,1024]{1,0:T(8,128)(2,1)}, f32[2048,1024]{1,0:T(8,128)}) custom-call(s32[32]{0:T(128)S(1)} %convert_element_type.9.present_ref, s32[8]{0:T(128)S(1)} %dynamic_slice.9.row_count_ref, s32[4]{0:T(128)S(1)} %dynamic_slice.10.col_count_ref, bf16[2048,128]{1,0:T(8,128)(2,1)S(1)} %copy-done.1, ...), custom_call_target="tpu_custom_call" | custom-call | flops 6442450944 | bytes 12582912 | tf_op jit(solution)/shard_map/finish/pallas_call | solution.py:249
  (50 shorter events, 5.3 us)
Async XLA Ops:
  7.2 4.3 copy-start
  7.2 60.7 %all-reduce.4.cloned.1.call-start = ((), (), s32[]{:S(2)}) async-start(), calls=%async_computation.4 | async-start | bytes 524288 | tf_op jit(solution)/shard_map/psum | solution.py:276
  11.4 101.4 %reduce-scatter.3.cloned.1.call-start = ((), (), s32[]{:S(2)}) async-start(), calls=%async_computation.3 | async-start | bytes 2359296 | tf_op jit(solution)/shard_map/reduce_scatter | solution.py:277
  19.3 124.4 %all-gather.7.cloned.1.call-start = ((), (), s32[]{:S(2)}) async-start(), calls=%async_computation.5 | async-start | bytes 2359296 | tf_op jit(solution)/shard_map/all_gather | solution.py:295
  67.9 0.9 copy-start.10
  112.8 0.9 copy-start.3
  115.6 158.4 %all-reduce.6.cloned.1.call-start = ((), (), s32[]{:S(2)}) async-start(), calls=%async_computation.7 | async-start | bytes 524288 | tf_op jit(solution)/shard_map/psum | solution.py:294
  116.2 186.8 %reduce-scatter.5.cloned.1.call-start = ((), (), s32[]{:S(2)}) async-start(), calls=%async_computation.6 | async-start | bytes 1310720 | tf_op jit(solution)/shard_map/reduce_scatter | solution.py:296
  143.7 1.6 copy-start.4
  145.2 6.3 %copy-start.11 = (bf16[2048,128]{1,0:T(8,128)(2,1)S(1)}, bf16[2048,128]{1,0:T(8,128)(2,1)}, u32[]{:S(2)}) copy-start(bf16[2048,128]{1,0:T(8,128)(2,1)} %param.5) | copy-start | bytes 1572868
  151.5 198.2 %all-gather.5.cloned.1.call-start = ((), (), s32[]{:S(2)}) async-start(), calls=%async_computation.2 | async-start | bytes 2621440 | tf_op jit(solution)/shard_map/all_gather | solution.py:283
  153.0 153.5 %copy-start.13 = (s32[32]{0:T(128)S(1)}, s32[32]{0:T(128)}, u32[]{:S(2)}) copy-start(s32[32]{0:T(128)} %param.6) | copy-start | bytes 388
  153.0 153.6 %copy-start.12 = (s32[8,2]{0,1:T(2,128)S(1)}, s32[8,2]{0,1:T(2,128)}, u32[]{:S(2)}) copy-start(s32[8,2]{0,1:T(2,128)} %param.7) | copy-start | bytes 196
  153.0 326.8 %all-reduce.8.cloned.1.call-start = ((), (), s32[]{:S(2)}) async-start(), calls=%async_computation.9 | async-start | bytes 524288 | tf_op jit(solution)/shard_map/psum | solution.py:298
  274.0 0.9 copy-start.7
  275.0 204.8 %copy-start.8 = (f32[256,256]{1,0:T(8,128)S(1)}, f32[256,256]{1,0:T(8,128)}, u32[]{:S(2)}) copy-start(f32[256,256]{1,0:T(8,128)} %all-reduce.6.cloned.1.call-done.gram_ref.gram_left_ref) | copy-start | bytes 786436
  302.9 0.9 copy-start.2
  305.7 205.6 %all-gather.9.cloned.1.call-start = ((), (), s32[]{:S(2)}) async-start(), calls=%async_computation.8 | async-start | bytes 1310720 | tf_op jit(solution)/shard_map/all_gather | solution.py:299
  350.7 160.7 %copy-start.1 = (bf16[2048,128]{1,0:T(8,128)(2,1)S(1)}, bf16[2048,128]{1,0:T(8,128)(2,1)}, u32[]{:S(2)}) copy-start(bf16[2048,128]{1,0:T(8,128)(2,1)} %fusion.1.row_unit_ref) | copy-start | bytes 1572868
  350.7 160.7 %copy-start.5 = (bf16[2048,512]{1,0:T(8,128)(2,1)S(1)}, bf16[2048,512]{1,0:T(8,128)(2,1)}, u32[]{:S(2)}) copy-start(bf16[2048,512]{1,0:T(8,128)(2,1)} %all-gather.7.cloned.1.call-done.left_ref) | copy-start | bytes 6291460
  479.8 1.0 copy-start.9
  511.3 1.2 copy-start.6
Sparse Core Ops, SparseCore 0:
  11.6 56.2 all-reduce.3
  72.1 40.6 reduce-scatter.2
  115.7 27.8 all-gather.6
  149.0 124.9 all-reduce.5
  276.8 26.1 reduce-scatter.4
  305.0 44.6 all-gather.4
  356.1 123.6 all-reduce.7
  482.0 29.2 all-gather.8

commit v2 on v1

--- a/solution.py
+++ b/solution.py
@@ -266,37 +266,280 @@
     )(present, row_count, col_count, row_unit, col_unit, left_pair, right_pair, mix)
 
 
+MESH = pl.DeviceIdType.MESH
+
+
+def greet(peers):
+    barrier = pltpu.get_barrier_semaphore()
+    for peer in peers:
+        pl.semaphore_signal(barrier, inc=1, device_id=peer, device_id_type=MESH)
+    pl.semaphore_wait(barrier, len(peers))
+
+
+def ring_place(place, step, total):
+    return lax.rem(place + step, total)
+
+
+def sum_body(
+    over_rows, row_total, col_total,
+    part_ref, out_ref, extra_ref,
+    col_in, row_in, spread, send_col, recv_col, send_row, recv_row, send_out, recv_out,
+):
+    row, col = lax.axis_index("row"), lax.axis_index("col")
+    piece = spread.shape[1]
+    cols = [(row, ring_place(col, k, col_total)) for k in range(1, col_total)]
+    rows = [(ring_place(row, k, row_total), col) for k in range(1, row_total)] if over_rows else []
+    greet(cols + rows)
+    copies = []
+    for k in range(1, col_total):
+        copy = pltpu.make_async_remote_copy(
+            src_ref=part_ref.at[cols[k - 1][1]], dst_ref=col_in.at[k - 1],
+            send_sem=send_col.at[k - 1], recv_sem=recv_col.at[k - 1],
+            device_id=cols[k - 1], device_id_type=MESH,
+        )
+        copy.start()
+        copies.append(copy)
+    total = part_ref[col]
+    for k in range(1, col_total):
+        copies[k - 1].wait_recv()
+        total = total + col_in[k - 1]
+    if extra_ref.shape[0] != 0:
+        extra_ref[...] = total[piece:, :]
+        total = total[:piece, :]
+    if over_rows:
+        row_in[row] = total
+        for k in range(1, row_total):
+            copy = pltpu.make_async_remote_copy(
+                src_ref=row_in.at[row], dst_ref=row_in.at[row],
+                send_sem=send_row.at[k - 1], recv_sem=recv_row.at[k - 1],
+                device_id=rows[k - 1], device_id_type=MESH,
+            )
+            copy.start()
+            copies.append(copy)
+        for copy in copies[col_total - 1:]:
+            copy.wait_recv()
+        total = row_in[0]
+        for k in range(1, row_total):
+            total = total + row_in[k]
+    spread[col] = total
+    last = []
+    for k in range(1, col_total):
+        copy = pltpu.make_async_remote_copy(
+            src_ref=spread.at[col], dst_ref=spread.at[col],
+            send_sem=send_out.at[k - 1], recv_sem=recv_out.at[k - 1],
+            device_id=cols[k - 1], device_id_type=MESH,
+        )
+        copy.start()
+        last.append(copy)
+    for copy in last:
+        copy.wait_recv()
+    out_ref[...] = spread[...]
+    for copy in copies + last:
+        copy.wait_send()
+
+
+def sum_everywhere(part, extra, over_rows, call_id, name):
+    n = part.shape[0]
+    row_total, col_total = lax.axis_size("row"), lax.axis_size("col")
+    piece = n // col_total
+    stacked = jnp.concatenate([part.reshape(col_total, piece, n), extra], axis=1)
+    dma = pltpu.SemaphoreType.DMA
+    total, rest = pl.pallas_call(
+        functools.partial(sum_body, over_rows, row_total, col_total),
+        in_specs=[pl.BlockSpec(memory_space=pltpu.VMEM)],
+        out_specs=(pl.BlockSpec(memory_space=pltpu.VMEM),) * 2,
+        out_shape=(
+            jax.ShapeDtypeStruct((col_total, piece, n), F32),
+            jax.ShapeDtypeStruct((extra.shape[1], n), F32),
+        ),
+        scratch_shapes=[
+            pltpu.VMEM((col_total - 1, piece + extra.shape[1], n), F32),
+            pltpu.VMEM((row_total, piece, n), F32),
+            pltpu.VMEM((col_total, piece, n), F32),
+            dma((col_total - 1,)), dma((col_total - 1,)),
+            dma((row_total - 1,)), dma((row_total - 1,)),
+            dma((col_total - 1,)), dma((col_total - 1,)),
+        ],
+        compiler_params=pltpu.CompilerParams(
+            vmem_limit_bytes=48 * 1024 * 1024, collective_id=call_id, has_side_effects=True
+        ),
+        name=name,
+        cost_estimate=pl.CostEstimate(flops=n * n * 10, bytes_accessed=40 * n * n, transcendentals=0),
+    )(stacked)
+    return total.reshape(n, n), rest
+
+
+def chip_peers(col_total):
+    row, col = lax.axis_index("row"), lax.axis_index("col")
+    core = lax.rem(col, 2)
+    chips = col_total // 2
+    chip = col // 2
+    sibling = (row, col + 1 - 2 * core)
+    ahead = [(row, 2 * ring_place(chip, k, chips) + core) for k in range(1, chips)]
+    return row, col, core, chip, chips, sibling, ahead
+
+
+def reduce_body(col_total, terms_ref, out_ref, from_core, joined, from_chip, send_core, recv_core, send_chip, recv_chip):
+    row, col, core, chip, chips, sibling, ahead = chip_peers(col_total)
+    greet([sibling] + ahead)
+    order = list(range(1, chips)) + [0]
+    near, far = {}, {}
+    for k in order:
+        copy = pltpu.make_async_remote_copy(
+            src_ref=terms_ref.at[2 * ring_place(chip, k, chips) + 1 - core], dst_ref=from_core.at[k],
+            send_sem=send_core.at[k], recv_sem=recv_core.at[k], device_id=sibling, device_id_type=MESH,
+        )
+        copy.start()
+        near[k] = copy
+    for k in order[:-1]:
+        near[k].wait_recv()
+        joined[k - 1] = terms_ref[2 * ring_place(chip, k, chips) + core] + from_core[k]
+        copy = pltpu.make_async_remote_copy(
+            src_ref=joined.at[k - 1], dst_ref=from_chip.at[k - 1],
+            send_sem=send_chip.at[k - 1], recv_sem=recv_chip.at[k - 1],
+            device_id=ahead[k - 1], device_id_type=MESH,
+        )
+        copy.start()
+        far[k] = copy
+    near[0].wait_recv()
+    total = terms_ref[col] + from_core[0]
+    for k in order[:-1]:
+        far[k].wait_recv()
+        total = total + from_chip[k - 1]
+    out_ref[...] = total
+    for copy in list(near.values()) + list(far.values()):
+        copy.wait_send()
+
+
+def reduce_over_col(terms, call_id):
+    rows, rank = terms.shape
+    col_total = lax.axis_size("col")
+    chips = col_total // 2
+    piece = rows // col_total
+    dma = pltpu.SemaphoreType.DMA
+    return pl.pallas_call(
+        functools.partial(reduce_body, col_total),
+        in_specs=[pl.BlockSpec(memory_space=pltpu.VMEM)],
+        out_specs=pl.BlockSpec(memory_space=pltpu.VMEM),
+        out_shape=jax.ShapeDtypeStruct((piece, rank), F32),
+        scratch_shapes=[
+            pltpu.VMEM((chips, piece, rank), F32),
+            pltpu.VMEM((chips - 1, piece, rank), F32),
+            pltpu.VMEM((chips - 1, piece, rank), F32),
+            dma((chips,)), dma((chips,)), dma((chips - 1,)), dma((chips - 1,)),
+        ],
+        compiler_params=pltpu.CompilerParams(
+            vmem_limit_bytes=48 * 1024 * 1024, collective_id=call_id, has_side_effects=True
+        ),
+        name="left_reduce",
+        cost_estimate=pl.CostEstimate(flops=rows * rank, bytes_accessed=40 * rows * rank, transcendentals=0),
+    )(terms.reshape(col_total, piece, rank))
+
+
+def gather_body(col_total, piece_ref, out_ref, held, send_core, recv_core, send_chip, recv_chip):
+    row, col, core, chip, chips, sibling, ahead = chip_peers(col_total)
+    held[col] = piece_ref[...]
+    greet([sibling] + ahead)
+
+    def send(slot, target, send_sem, recv_sem):
+        copy = pltpu.make_async_remote_copy(
+            src_ref=held.at[slot], dst_ref=held.at[slot], send_sem=send_sem, recv_sem=recv_sem,
+            device_id=target, device_id_type=MESH,
+        )
+        copy.start()
+        return copy
+
+    far = [send(col, ahead[k - 1], send_chip.at[k - 1], recv_chip.at[k - 1]) for k in range(1, chips)]
+    near = [send(col, sibling, send_core.at[0], recv_core.at[0])]
+    for k in range(1, chips):
+        far[k - 1].wait_recv()
+        source = 2 * ring_place(chip, chips - k, chips) + core
+        near.append(send(source, sibling, send_core.at[k], recv_core.at[k]))
+    for copy in near:
+        copy.wait_recv()
+    out_ref[...] = held[...]
+    for copy in near + far:
+        copy.wait_send()
+
+
+def gather_over_col(piece, call_id):
+    rows, width = piece.shape
+    col_total = lax.axis_size("col")
+    chips = col_total // 2
+    dma = pltpu.SemaphoreType.DMA
+    whole = pl.pallas_call(
+        functools.partial(gather_body, col_total),
+        in_specs=[pl.BlockSpec(memory_space=pltpu.VMEM)],
+        out_specs=pl.BlockSpec(memory_space=pltpu.VMEM),
+        out_shape=jax.ShapeDtypeStruct((col_total, rows, width), piece.dtype),
+        scratch_shapes=[
+            pltpu.VMEM((col_total, rows, width), piece.dtype),
+            dma((chips,)), dma((chips,)), dma((chips - 1,)), dma((chips - 1,)),
+        ],
+        compiler_params=pltpu.CompilerParams(
+            vmem_limit_bytes=48 * 1024 * 1024, collective_id=call_id, has_side_effects=True
+        ),
+        name="left_gather",
+        cost_estimate=pl.CostEstimate(flops=rows, bytes_accessed=80 * rows * width, transcendentals=0),
+    )(piece)
+    return whole.reshape(col_total * rows, width)
+
+
+def own_columns(unit, cols):
+    rows = unit.shape[0]
+    row_total, col_total = lax.axis_size("row"), lax.axis_size("col")
+    start = lax.axis_index("col") * cols
+    held = lax.dynamic_slice_in_dim(unit, lax.rem(start, rows), cols, 0)
+    found = jnp.where(start // rows == lax.axis_index("row"), held, jnp.zeros_like(held))
+    for k in range(1, row_total):
+        pairs = []
+        for place in range(col_total):
+            owner = place * cols // rows
+            pairs.append((owner * col_total + place, (owner + k) % row_total * col_total + place))
+        found = found + lax.ppermute(held, ("row", "col"), pairs)
+    return found
+
+
 def local(descriptors, image_counts, pair_list, warm_start, factor_init):
     row_place = lax.axis_index("row")
     col_place = lax.axis_index("col")
     rows, cols = warm_start.shape
     img_row, img_col = rows // KP, cols // KP
 
+    row_total, col_total = lax.axis_size("row"), lax.axis_size("col")
+    rank = factor_init.shape[1]
+
+    cells = img_row * img_col
+    codes = (pair_list[:, 0] - img_row * row_place) * img_col + lax.rem(pair_list[:, 1], img_col)
+    hits = (pair_list[:, 1] // img_col)[:, None] == jnp.arange(col_total, dtype=jnp.int32)[None, :]
+    marks = codes[:, None] == jnp.arange(cells, dtype=jnp.int32)[None, :]
+    flags = jnp.any(hits[:, :, None] & marks[:, None, :], axis=0).astype(F32)
+    flags = jnp.pad(flags[:, None, :], ((0, 0), (0, 7), (0, rank - cells)))
+    blank = jnp.zeros((col_total, 8, rank), F32)
+
     left_terms = left_sum(warm_start, factor_init)
-    gram_right = lax.psum(lax.dot_general(factor_init, factor_init, (((0,), (0,)), ((), ())), precision=EXACT), "col")
-    left_terms = lax.psum_scatter(left_terms, "col", scatter_dimension=0, tiled=True)
+    gram_right = lax.dot_general(factor_init, factor_init, (((0,), (0,)), ((), ())), precision=EXACT)
+    gram_right, listed = sum_everywhere(gram_right, flags, False, 1, "start_gram")
+    present = (listed[0, :cells] > 0.5).astype(jnp.int32)
+    left_terms = reduce_over_col(left_terms, 2)
 
     wide = descriptors.astype(F32)
     unit = (
         wide * lax.rsqrt(descriptors.shape[1] * (jnp.mean(wide * wide, axis=1, keepdims=True) + EPSILON))
     ).astype(BF16)
-    everyone = lax.all_gather(unit, "row", axis=0, tiled=True)
-    col_unit = lax.dynamic_slice_in_dim(everyone, col_place * cols, cols, 0)
-    listed = lax.all_gather(pair_list, "col", axis=0, tiled=True)
-    in_block = listed[:, 1] // img_col == col_place
-    local_code = (listed[:, 0] - img_row * row_place) * img_col + (listed[:, 1] - img_col * col_place)
-    cell_iota = jnp.arange(img_row * img_col, dtype=jnp.int32)
-    present = jnp.any((local_code[:, None] == cell_iota[None, :]) & in_block[:, None], axis=0).astype(jnp.int32)
+    col_unit = own_columns(unit, cols)
     row_count = lax.dynamic_slice_in_dim(image_counts, row_place * img_row, img_row, 0)
     col_count = lax.dynamic_slice_in_dim(image_counts, col_place * img_col, img_col, 0)
 
     left_pair, gram_left = left_apply(left_terms, ridge_inverse(gram_right))
-    gram_left = lax.psum(gram_left, ("row", "col"))
-    left_pair = lax.all_gather(left_pair, "col", axis=0, tiled=True)
-    right_terms = lax.psum_scatter(right_sum(left_pair, warm_start), "row", scatter_dimension=1, tiled=True)
+    left_pair = gather_over_col(left_pair, 3)
+    right_terms = right_sum(left_pair, warm_start)
+    gram_left, right_terms = lax.optimization_barrier((gram_left, right_terms))
+    right_terms = lax.psum_scatter(right_terms, "row", scatter_dimension=1, tiled=True)
+    gram_left = sum_everywhere(gram_left, blank, True, 4, "left_gram")[0]
     right_pair, gram_right = right_apply(right_terms, ridge_inverse(gram_left))
-    gram_right = lax.psum(gram_right, ("row", "col"))
     right_pair = lax.all_gather(right_pair, "row", axis=1, tiled=True)
+    gram_right = sum_everywhere(gram_right, blank, True, 5, "right_gram")[0]
     mix = second_mix(gram_right, gram_left)
     return finish(present, row_count, col_count, unit, col_unit, left_pair, right_pair, mix)
 

time: 540 us -> 221 us (0.41)
  waiting for transfers between devices: 424 us -> 22.9 us
  Pallas kernels: 75.1 us -> 160 us
  starting transfers between devices: 0.33 us -> 9.72 us
  blocking collectives: 8.85 us -> 0 us
    psum x3 -> x0, waiting for transfers between devices: 299 us -> none  [the longest x1 129 us: local(): gram_right = lax.psum(gram_right, ('row', 'col'))]
    pallas_call x0 -> x5, Pallas kernels: none -> 87.3 us  [the longest x3 54.5 us: sum_everywhere(): pl.pallas_call(functools.partial(sum_body, over_rows, row_total, col_tota...]
    all_gather x2 -> x0, waiting for transfers between devices: 61.4 us -> none  [the longest x1 34 us: local(): everyone = lax.all_gather(unit, 'row', axis=0, tiled=True)]
    reduce_scatter x2 -> x1, waiting for transfers between devices: 53.7 us -> 0.02 us  [local(): lax.psum_scatter(right_terms, 'row', scatter_dimension=1, tiled=True)]
    ppermute x0 -> x3, waiting for transfers between devices: none -> 22.8 us  [own_columns(): found = found + lax.ppermute(held, ('row', 'col'), pairs)]
    ppermute x0 -> x3, starting transfers between devices: none -> 9.64 us  [own_columns(): found = found + lax.ppermute(held, ('row', 'col'), pairs)]
    all_gather x1, waiting for transfers between devices: 9.32 us -> 0.01 us  [local(): right_pair = lax.all_gather(right_pair, 'row', axis=1, tiled=True)]
    all_gather x1 -> x0, blocking collectives: 8.85 us -> none  [local(): listed = lax.all_gather(pair_list, 'col', axis=0, tiled=True)]
  transfers between devices with their start and end apart: 8 -> 5, of which waited for: 8 -> 3; matrix products, arithmetic and copies ran while one was open for 1% -> 1% of each run, Pallas kernels for 10% -> 33%
where the time goes in v2:
time: 221 us; the launch traced here: 218 us
  Pallas kernels  160 us (72%)
  waiting for transfers between devices  22.9 us (10%)
  between operations  14.3 us (6%)
  starting transfers between devices  9.72 us (4%)
  local copies, waits for them, and re-layouts  4.06 us (2%)
  other arithmetic  4.03 us (2%)
  matrix products  3.39 us (2%)
    pallas_call x3, Pallas kernels, sum_everywhere(): pl.pallas_call(functools.partial(sum_body, over_rows, row_total, col_tota...  54.5 us
    ppermute x3, waiting for transfers between devices, own_columns(): found = found + lax.ppermute(held, ('row', 'col'), pairs)  22.8 us
    pallas_call x1, Pallas kernels, second_mix(): pl.pallas_call(second_body, out_shape=jax.ShapeDtypeStruct((n, n), F32),...  21.2 us
    pallas_call x2, Pallas kernels, ridge_inverse(): pl.pallas_call(inverse_body, out_shape=jax.ShapeDtypeStruct(gram.shape, F...  18.2 us
    pallas_call x1, Pallas kernels, finish(): pl.pallas_call(functools.partial(finish_body, img_col), grid=(rows // KP,...  18.1 us
    pallas_call x1, Pallas kernels, reduce_over_col(): pl.pallas_call(functools.partial(reduce_body, col_total), in_specs=[pl.Bl...  16.8 us
    pallas_call x1, Pallas kernels, gather_over_col(): pl.pallas_call(functools.partial(gather_body, col_total), in_specs=[pl.Bl...  15.9 us
    ppermute x3, starting transfers between devices, own_columns(): found = found + lax.ppermute(held, ('row', 'col'), pairs)  9.64 us
  transfers between devices with their start and end apart: 5, of which 3 were waited for; matrix products, arithmetic and copies ran while one was open for 1% of the time, Pallas kernels for 33%

profile of v2, /device:TPU:0, one launch (start us, length us, event | category | flops | bytes accessed | tf_op | source)
XLA Modules:
  0.0 218.4 jit_solution(4548756132047363746)
XLA Ops:
  8.3 3.4 %fusion.4 = f32[256,256]{1,0:T(8,128)S(1)} fusion(f32[1024,256]{1,0:T(8,128)} %right_ref.1), kind=kOutput, calls=%fused_computation.20 | convolution fusion | flops 805306368 | bytes 1310720 | tf_op jit(solution)/shard_map/dot_general | solution.py:521
  11.7 14.0 %start_gram.1 = (f32[8,32,256]{2,1,0:T(8,128)S(1)}, f32[8,256]{1,0:T(8,128)S(1)}) custom-call(f32[8,40,256]{2,1,0:T(8,128)S(1)} %pad_maximum_fusion.part_ref), custom_call_target="tpu_custom_call" | custom-call | flops 655360 | bytes 2621440 | tf_op jit(solution)/shard_map/start_gram/pallas_call | solution.py:347
  25.7 8.0 %ridge_inverse.2.inverse_ref = f32[256,256]{1,0:T(8,128)S(1)} custom-call(f32[256,256]{1,0:T(8,128)S(1)} %bitcast.25), custom_call_target="tpu_custom_call" | custom-call | flops 3355443200 | bytes 524288 | tf_op jit(solution)/shard_map/ridge_inverse/pallas_call | solution.py:62
  33.7 6.7 %left_sum.1 = f32[2048,256]{1,0:T(8,128)S(1)} custom-call(bf16[2048,1024]{1,0:T(8,128)(2,1)} %warm_ref.3, f32[1024,256]{1,0:T(8,128)S(1)} %copy-done), custom_call_target="tpu_custom_call" | custom-call | flops 2147483648 | bytes 4194304 | tf_op jit(solution)/shard_map/left_sum/pallas_call | solution.py:106
  40.4 16.8 %left_reduce.1.terms_ref = f32[256,256]{1,0:T(8,128)S(1)} custom-call(f32[8,256,256]{2,1,0:T(8,128)S(1)} %bitcast.19), custom_call_target="tpu_custom_call" | custom-call | flops 524288 | bytes 20971520 | tf_op jit(solution)/shard_map/left_reduce/pallas_call | solution.py:420
  57.2 1.1 left_apply.1
  58.3 15.9 %left_gather.1 = bf16[8,256,512]{2,1,0:T(8,128)(2,1)S(1)} custom-call(bf16[256,512]{1,0:T(8,128)(2,1)S(1)} %get-tuple-element.14.piece_ref), custom_call_target="tpu_custom_call" | custom-call | flops 256 | bytes 10485760 | tf_op jit(solution)/shard_map/left_gather/pallas_call | solution.py:470
  74.3 6.2 %right_sum.1 = f32[256,1024]{1,0:T(8,128)} custom-call(bf16[2048,512]{1,0:T(8,128)(2,1)S(1)} %bitcast.17, bf16[2048,1024]{1,0:T(8,128)(2,1)} %warm_ref.3), custom_call_target="tpu_custom_call" | custom-call | flops 2147483648 | bytes 4194304 | tf_op jit(solution)/shard_map/right_sum/pallas_call | solution.py:135
  80.6 21.0 %left_gram.1 = (f32[8,32,256]{2,1,0:T(8,128)S(1)}, f32[8,256]{1,0:T(8,128)}) custom-call(f32[8,40,256]{2,1,0:T(8,128)S(1)} %concatenate.10.part_ref), custom_call_target="tpu_custom_call" | custom-call | flops 655360 | bytes 2621440 | tf_op jit(solution)/shard_map/left_gram/pallas_call | solution.py:347
  102.0 10.2 %ridge_inverse.3.inverse_ref = f32[256,256]{1,0:T(8,128)S(1)} custom-call(f32[256,256]{1,0:T(8,128)S(1)} %bitcast.22), custom_call_target="tpu_custom_call" | custom-call | flops 3355443200 | bytes 524288 | tf_op jit(solution)/shard_map/ridge_inverse/pallas_call | solution.py:62
  112.2 0.9 copy-done.1
  113.2 1.3 right_apply.1
  114.4 1.4 fusion.1.row_unit_ref
  115.9 3.4 %collective-permute-start.1 = (bf16[1024,128]{1,0:T(8,128)(2,1)S(1)}, bf16[1024,128]{1,0:T(8,128)(2,1)}, u32[]{:S(2)}, u32[]{:S(2)}) collective-permute-start(bf16[1024,128]{1,0:T(8,128)(2,1)S(1)} %constant_dynamic-slice_fusion), channel_id=1, source_target_pairs={{0,16},{1,17},{10,26},{11,27},{20,4},{21,5},{30,14},{31,15}} | collective-permute-start | bytes 786440 | tf_op jit(solution)/shard_map/ppermute | solution.py:499
  119.3 3.1 %collective-permute-start = (bf16[1024,128]{1,0:T(8,128)(2,1)S(1)}, bf16[1024,128]{1,0:T(8,128)(2,1)}, u32[]{:S(2)}, u32[]{:S(2)}) collective-permute-start(bf16[1024,128]{1,0:T(8,128)(2,1)S(1)} %constant_dynamic-slice_fusion), channel_id=1, source_target_pairs={{0,8},{1,9},{10,18},{11,19},{20,28},{21,29},{30,6},{31,7}} | collective-permute-start | bytes 786440 | tf_op jit(solution)/shard_map/ppermute | solution.py:499
  122.3 3.2 %collective-permute-start.2 = (bf16[1024,128]{1,0:T(8,128)(2,1)S(1)}, bf16[1024,128]{1,0:T(8,128)(2,1)}, u32[]{:S(2)}, u32[]{:S(2)}) collective-permute-start(bf16[1024,128]{1,0:T(8,128)(2,1)S(1)} %constant_dynamic-slice_fusion), channel_id=1, source_target_pairs={{0,24},{1,25},{10,2},{11,3},{20,12},{21,13},{30,22},{31,23}} | collective-permute-start | bytes 786440 | tf_op jit(solution)/shard_map/ppermute | solution.py:499
  126.3 11.2 %collective-permute-done = bf16[1024,128]{1,0:T(8,128)(2,1)} collective-permute-done((bf16[1024,128]{1,0:T(8,128)(2,1)S(1)}, bf16[1024,128]{1,0:T(8,128)(2,1)}, u32[]{:S(2)}, u32[]{:S(2)}) %collective-permute-start) | collective-permute-done | bytes 262176 | tf_op jit(solution)/shard_map/ppermute | solution.py:499
  137.5 10.9 %collective-permute-done.2 = bf16[1024,128]{1,0:T(8,128)(2,1)} collective-permute-done((bf16[1024,128]{1,0:T(8,128)(2,1)S(1)}, bf16[1024,128]{1,0:T(8,128)(2,1)}, u32[]{:S(2)}, u32[]{:S(2)}) %collective-permute-start.2) | collective-permute-done | bytes 262176 | tf_op jit(solution)/shard_map/ppermute | solution.py:499
  148.5 1.3 add_add_fusion.col_unit_ref
  149.8 19.5 %right_gram.1 = (f32[8,32,256]{2,1,0:T(8,128)S(1)}, f32[8,256]{1,0:T(8,128)}) custom-call(f32[8,40,256]{2,1,0:T(8,128)S(1)} %concatenate.11.part_ref), custom_call_target="tpu_custom_call" | custom-call | flops 655360 | bytes 2621440 | tf_op jit(solution)/shard_map/right_gram/pallas_call | solution.py:347
  169.3 21.2 %second_mix.1.mix_ref = f32[256,256]{1,0:T(8,128)S(1)} custom-call(f32[256,256]{1,0:T(8,128)S(1)} %bitcast.24, f32[256,256]{1,0:T(8,128)S(1)} %bitcast.23), custom_call_target="tpu_custom_call" | custom-call | flops 6710886400 | bytes 786432 | tf_op jit(solution)/shard_map/second_mix/pallas_call | solution.py:85
  191.3 1.2 copy-done.2
  192.5 0.9 copy-done.4
  193.4 18.1 %finish.1 = (bf16[2048,1024]{1,0:T(8,128)(2,1)}, f32[2048,1024]{1,0:T(8,128)}) custom-call(s32[32]{0:T(128)S(1)} %fusion.2.present_ref, s32[8]{0:T(128)S(1)} %dynamic_slice.9.row_count_ref, s32[4]{0:T(128)S(1)} %dynamic_slice.10.col_count_ref, bf16[2048,128]{1,0:T(8,128)(2,1)S(1)} %fusion.1.row_unit_ref, bf16[1024,128]{1,0:T(8,128)(2,1)S(1)} %add_add_fusion.col_unit_ref, ...), custom_call_target="tpu_custom_call" | custom-call | flops 6442450944 | bytes 12582912 | tf_op jit(solution)/shard_map/finish/pallas_call | solution.py:249
  (33 shorter events, 3.1 us)
Async XLA Ops:
  7.2 105.0 %reduce-scatter.2.cloned.1.call-start = ((), (), s32[]{:S(2)}) async-start(), calls=%async_computation.1 | async-start | bytes 1310720 | tf_op jit(solution)/shard_map/reduce_scatter | solution.py:538
  25.7 8.0 %copy-start = (f32[1024,256]{1,0:T(8,128)S(1)}, f32[1024,256]{1,0:T(8,128)}, u32[]{:S(2)}) copy-start(f32[1024,256]{1,0:T(8,128)} %right_ref.1) | copy-start | bytes 3145732
  74.2 27.3 %copy-start.5 = (bf16[2048,128]{1,0:T(8,128)(2,1)S(1)}, bf16[2048,128]{1,0:T(8,128)(2,1)}, u32[]{:S(2)}) copy-start(bf16[2048,128]{1,0:T(8,128)(2,1)} %param.5) | copy-start | bytes 1572868
  80.5 110.8 %all-gather.2.cloned.1.call-start = ((), (), s32[]{:S(2)}) async-start(), calls=%async_computation.2 | async-start | bytes 1310720 | tf_op jit(solution)/shard_map/all_gather | solution.py:541
  101.9 23.6 %copy-start.6 = (s32[32]{0:T(128)S(1)}, s32[32]{0:T(128)}, u32[]{:S(2)}) copy-start(s32[32]{0:T(128)} %param.6) | copy-start | bytes 388
  112.2 1.0 copy-start.1
  115.9 10.4 %collective-permute-start.1 = (bf16[1024,128]{1,0:T(8,128)(2,1)S(1)}, bf16[1024,128]{1,0:T(8,128)(2,1)}, u32[]{:S(2)}, u32[]{:S(2)}) collective-permute-start(bf16[1024,128]{1,0:T(8,128)(2,1)S(1)} %constant_dynamic-slice_fusion), channel_id=1, source_target_pairs={{0,16},{1,17},{10,26},{11,27},{20,4},{21,5},{30,14},{31,15}} | collective-permute-start | bytes 786440 | tf_op jit(solution)/shard_map/ppermute | solution.py:499
  119.3 18.3 %collective-permute-start = (bf16[1024,128]{1,0:T(8,128)(2,1)S(1)}, bf16[1024,128]{1,0:T(8,128)(2,1)}, u32[]{:S(2)}, u32[]{:S(2)}) collective-permute-start(bf16[1024,128]{1,0:T(8,128)(2,1)S(1)} %constant_dynamic-slice_fusion), channel_id=1, source_target_pairs={{0,8},{1,9},{10,18},{11,19},{20,28},{21,29},{30,6},{31,7}} | collective-permute-start | bytes 786440 | tf_op jit(solution)/shard_map/ppermute | solution.py:499
  122.3 26.1 %collective-permute-start.2 = (bf16[1024,128]{1,0:T(8,128)(2,1)S(1)}, bf16[1024,128]{1,0:T(8,128)(2,1)}, u32[]{:S(2)}, u32[]{:S(2)}) collective-permute-start(bf16[1024,128]{1,0:T(8,128)(2,1)S(1)} %constant_dynamic-slice_fusion), channel_id=1, source_target_pairs={{0,24},{1,25},{10,2},{11,3},{20,12},{21,13},{30,22},{31,23}} | collective-permute-start | bytes 786440 | tf_op jit(solution)/shard_map/ppermute | solution.py:499
  190.6 0.7 copy-start.3
  191.3 1.2 copy-start.2
  192.5 0.9 copy-start.4
Sparse Core Ops, SparseCore 0:
  80.6 30.1 reduce-scatter.1
  114.6 38.4 all-gather.1

commit v3 on v2

--- a/solution.py
+++ b/solution.py
@@ -17,6 +17,7 @@
 BF16 = jnp.bfloat16
 PARAMS = pltpu.CompilerParams(vmem_limit_bytes=48 * 1024 * 1024)
 SETTLED = 2e-4
+ROUGH_TOP = 1000.0 * RIDGE
 
 
 def halves(x):
@@ -30,6 +31,12 @@
 
 def exact(a, b):
     return jnp.dot(a, b, precision=EXACT, preferred_element_type=F32)
+
+
+def rough_product(a, b):
+    a_high, a_low = halves(a)
+    b_high, b_low = halves(b)
+    return dot32(a_high, b_high) + dot32(a_high, b_low) + dot32(a_low, b_high)
 
 
 def eye(n):
@@ -40,17 +47,23 @@
 
 def invert(matrix_ref, inverse_ref):
     n = matrix_ref.shape[0]
-    top = jnp.max(jnp.sum(jnp.abs(matrix_ref[...]), axis=1, keepdims=True))
+    size = jnp.abs(matrix_ref[...])
+    top = jnp.max(jnp.sum(size, axis=1, keepdims=True))
+    top = jnp.minimum(top, 1.0001 * jnp.sqrt(jnp.sum(jnp.sum(size * size, axis=1, keepdims=True))))
+    top = jnp.maximum(top, 1.0001 * RIDGE)
     inverse_ref[...] = (2.0 / (RIDGE + top)) * eye(n)
 
-    def step(spread):
+    def step(product, spread):
         scale = 2.0 / (2.0 - spread * spread)
-        rest = (2.0 * scale) * eye(n) - scale * exact(matrix_ref[...], inverse_ref[...])
-        inverse_ref[...] = exact(inverse_ref[...], rest)
+        rest = (2.0 * scale) * eye(n) - scale * product(matrix_ref[...], inverse_ref[...])
+        inverse_ref[...] = product(inverse_ref[...], rest)
         return spread * spread / (2.0 - spread * spread)
 
-    spread = lax.while_loop(lambda s: s > SETTLED, step, (top - RIDGE) / (top + RIDGE))
-    step(spread)
+    spread = (top - RIDGE) / (top + RIDGE)
+    rough = jnp.where(top < ROUGH_TOP, 0.3, 2.0)
+    spread = lax.while_loop(lambda s: s > rough, functools.partial(step, rough_product), spread)
+    spread = lax.while_loop(lambda s: s > SETTLED, functools.partial(step, exact), spread)
+    step(exact, spread)
 
 
 def inverse_body(gram_ref, out_ref, matrix_ref):
@@ -186,23 +199,8 @@
     )(terms, inverse)
 
 
-def finish_body(
-    img_col,
-    present_ref, row_count_ref, col_count_ref,
-    row_unit_ref, col_unit_ref, left_ref, right_ref, mix_ref,
-    assign_ref, dual_ref,
-    second_ref, match_ref,
-):
-    rank = mix_ref.shape[0]
+def match_body(img_col, present_ref, row_count_ref, col_count_ref, row_unit_ref, col_unit_ref, match_ref):
     step = pl.program_id(0)
-
-    @pl.when(step == 0)
-    def _():
-        mix_high, mix_low = halves(mix_ref[...])
-        high, low = right_ref[:rank, :], right_ref[rank:, :]
-        mixed = dot32(mix_high, high) + dot32(mix_low, high) + dot32(mix_high, low)
-        second_ref[:rank, :], second_ref[rank:, :] = halves(mixed)
-
     row_valid = lax.broadcasted_iota(jnp.int32, (KP, 1), 0) < row_count_ref[step]
     for image in range(img_col):
         cell = slice(image * KP, (image + 1) * KP)
@@ -226,44 +224,71 @@
         def _():
             match_ref[:, cell] = jnp.zeros((KP, KP), F32)
 
-        left_high, left_low = left_ref[:, :rank], left_ref[:, rank:]
-
-        def product(ref):
-            high = ref[:rank, cell]
-            return dot32(left_high, high) + dot32(left_high, ref[rank:, cell]) + dot32(left_low, high)
-
-        half_match = match_ref[:, cell]
-        lowrank = product(right_ref)
-        half_dual = jnp.clip(lowrank + half_match, 0.0, 1.0) - lowrank
-        lowrank = product(second_ref)
-        solution = jnp.clip(lowrank + (half_match + half_dual), 0.0, 1.0)
-        dual_ref[:, cell] = 2.0 * (half_dual + (solution - lowrank))
-        assign_ref[:, cell] = solution.astype(BF16)
-
-
-def finish(present, row_count, col_count, row_unit, col_unit, left_pair, right_pair, mix):
-    rows, rank = left_pair.shape[0], mix.shape[0]
-    cols = right_pair.shape[1]
-    img_col = cols // KP
+
+def half_matches(present, row_count, col_count, row_unit, col_unit):
+    rows, cols = row_unit.shape[0], col_unit.shape[0]
     smem = pl.BlockSpec(memory_space=pltpu.SMEM)
     return pl.pallas_call(
-        functools.partial(finish_body, img_col),
+        functools.partial(match_body, cols // KP),
         grid=(rows // KP,),
         in_specs=[
             smem, smem, smem,
             pl.BlockSpec((KP, row_unit.shape[1]), lambda i: (i, 0)),
             pl.BlockSpec(col_unit.shape, lambda i: (0, 0)),
+        ],
+        out_specs=pl.BlockSpec((KP, cols), lambda i: (i, 0)),
+        out_shape=jax.ShapeDtypeStruct((rows, cols), F32),
+        compiler_params=PARAMS,
+        name="half_matches",
+        cost_estimate=pl.CostEstimate(flops=rows * cols * 256, bytes_accessed=4 * rows * cols, transcendentals=rows * cols),
+    )(present, row_count, col_count, row_unit, col_unit)
+
+
+def finish_body(img_col, match_ref, left_ref, right_ref, mix_ref, assign_ref, dual_ref, first_ref, second_ref):
+    rank = mix_ref.shape[0]
+
+    @pl.when(pl.program_id(0) == 0)
+    def _():
+        mix_high, mix_low = halves(mix_ref[...])
+        high, low = right_ref[:rank, :], right_ref[rank:, :]
+        first_ref[: 2 * rank, :] = right_ref[...]
+        first_ref[2 * rank :, :] = high
+        high, low = halves(dot32(mix_high, high) + dot32(mix_low, high) + dot32(mix_high, low))
+        second_ref[:rank, :] = high
+        second_ref[rank : 2 * rank, :] = low
+        second_ref[2 * rank :, :] = high
+
+    left = jnp.concatenate([left_ref[:, :rank], left_ref[...]], axis=1)
+    for image in range(img_col):
+        cell = slice(image * KP, (image + 1) * KP)
+        half_match = match_ref[:, cell]
+        lowrank = dot32(left, first_ref[:, cell])
+        half_dual = jnp.clip(lowrank + half_match, 0.0, 1.0) - lowrank
+        lowrank = dot32(left, second_ref[:, cell])
+        solution = jnp.clip(lowrank + (half_match + half_dual), 0.0, 1.0)
+        dual_ref[:, cell] = 2.0 * (half_dual + (solution - lowrank))
+        assign_ref[:, cell] = solution.astype(BF16)
+
+
+def finish(half_match, left_pair, right_pair, mix):
+    rows, rank = left_pair.shape[0], mix.shape[0]
+    cols = right_pair.shape[1]
+    return pl.pallas_call(
+        functools.partial(finish_body, cols // KP),
+        grid=(rows // KP,),
+        in_specs=[
+            pl.BlockSpec((KP, cols), lambda i: (i, 0)),
             pl.BlockSpec((KP, 2 * rank), lambda i: (i, 0)),
             pl.BlockSpec((2 * rank, cols), lambda i: (0, 0)),
             pl.BlockSpec((rank, rank), lambda i: (0, 0)),
         ],
         out_specs=(pl.BlockSpec((KP, cols), lambda i: (i, 0)), pl.BlockSpec((KP, cols), lambda i: (i, 0))),
         out_shape=(jax.ShapeDtypeStruct((rows, cols), BF16), jax.ShapeDtypeStruct((rows, cols), F32)),
-        scratch_shapes=[pltpu.VMEM((2 * rank, cols), BF16), pltpu.VMEM((KP, cols), F32)],
+        scratch_shapes=[pltpu.VMEM((3 * rank, cols), BF16)] * 2,
         compiler_params=PARAMS,
         name="finish",
-        cost_estimate=pl.CostEstimate(flops=12 * rows * cols * rank, bytes_accessed=6 * rows * cols, transcendentals=rows * cols),
-    )(present, row_count, col_count, row_unit, col_unit, left_pair, right_pair, mix)
+        cost_estimate=pl.CostEstimate(flops=12 * rows * cols * rank, bytes_accessed=10 * rows * cols, transcendentals=0),
+    )(half_match, left_pair, right_pair, mix)
 
 
 MESH = pl.DeviceIdType.MESH
@@ -280,93 +305,119 @@
     return lax.rem(place + step, total)
 
 
-def sum_body(
-    over_rows, row_total, col_total,
-    part_ref, out_ref, extra_ref,
-    col_in, row_in, spread, send_col, recv_col, send_row, recv_row, send_out, recv_out,
-):
-    row, col = lax.axis_index("row"), lax.axis_index("col")
-    piece = spread.shape[1]
-    cols = [(row, ring_place(col, k, col_total)) for k in range(1, col_total)]
-    rows = [(ring_place(row, k, row_total), col) for k in range(1, row_total)] if over_rows else []
-    greet(cols + rows)
-    copies = []
-    for k in range(1, col_total):
+def gram_scratch(row_total, col_total, piece, n):
+    dma = pltpu.SemaphoreType.DMA
+    return [
+        pltpu.VMEM((col_total - 1, piece + 8, n), F32),
+        pltpu.VMEM((row_total, piece, n), F32),
+        pltpu.VMEM((col_total, piece, n), F32),
+        dma((col_total - 1,)), dma((col_total - 1,)),
+        dma((row_total - 1,)), dma((row_total - 1,)),
+        dma((col_total - 1,)), dma((col_total - 1,)),
+    ]
+
+
+class GramSum:
+    def __init__(self, over_rows, row_total, col_total, part_ref, out_ref, extra_ref, scratch):
+        self.part_ref, self.out_ref, self.extra_ref = part_ref, out_ref, extra_ref
+        (self.col_in, self.row_in, self.spread, self.send_col, self.recv_col,
+         self.send_row, self.recv_row, self.send_out, self.recv_out) = scratch
+        self.row, self.col = lax.axis_index("row"), lax.axis_index("col")
+        self.cols = [(self.row, ring_place(self.col, k, col_total)) for k in range(1, col_total)]
+        self.rows = (
+            [(ring_place(self.row, k, row_total), self.col) for k in range(1, row_total)] if over_rows else []
+        )
+
+    def send(self, source, target, send_sem, recv_sem, peer):
         copy = pltpu.make_async_remote_copy(
-            src_ref=part_ref.at[cols[k - 1][1]], dst_ref=col_in.at[k - 1],
-            send_sem=send_col.at[k - 1], recv_sem=recv_col.at[k - 1],
-            device_id=cols[k - 1], device_id_type=MESH,
+            src_ref=source, dst_ref=target, send_sem=send_sem, recv_sem=recv_sem,
+            device_id=peer, device_id_type=MESH,
         )
         copy.start()
-        copies.append(copy)
-    total = part_ref[col]
-    for k in range(1, col_total):
-        copies[k - 1].wait_recv()
-        total = total + col_in[k - 1]
-    if extra_ref.shape[0] != 0:
-        extra_ref[...] = total[piece:, :]
-        total = total[:piece, :]
-    if over_rows:
-        row_in[row] = total
-        for k in range(1, row_total):
-            copy = pltpu.make_async_remote_copy(
-                src_ref=row_in.at[row], dst_ref=row_in.at[row],
-                send_sem=send_row.at[k - 1], recv_sem=recv_row.at[k - 1],
-                device_id=rows[k - 1], device_id_type=MESH,
-            )
-            copy.start()
-            copies.append(copy)
-        for copy in copies[col_total - 1:]:
+        return copy
+
+    def begin(self):
+        self.first = [
+            self.send(self.part_ref.at[peer[1]], self.col_in.at[k], self.send_col.at[k], self.recv_col.at[k], peer)
+            for k, peer in enumerate(self.cols)
+        ]
+
+    def add_cols(self):
+        piece = self.spread.shape[1]
+        total = self.part_ref[self.col]
+        for k, copy in enumerate(self.first):
             copy.wait_recv()
-        total = row_in[0]
-        for k in range(1, row_total):
-            total = total + row_in[k]
-    spread[col] = total
-    last = []
-    for k in range(1, col_total):
-        copy = pltpu.make_async_remote_copy(
-            src_ref=spread.at[col], dst_ref=spread.at[col],
-            send_sem=send_out.at[k - 1], recv_sem=recv_out.at[k - 1],
-            device_id=cols[k - 1], device_id_type=MESH,
-        )
-        copy.start()
-        last.append(copy)
-    for copy in last:
-        copy.wait_recv()
-    out_ref[...] = spread[...]
-    for copy in copies + last:
-        copy.wait_send()
-
-
-def sum_everywhere(part, extra, over_rows, call_id, name):
-    n = part.shape[0]
+            total = total + self.col_in[k]
+        self.extra_ref[...] = total[piece:, :]
+        self.row_in[self.row] = total[:piece, :]
+        mine = self.row_in.at[self.row]
+        self.second = [
+            self.send(mine, mine, self.send_row.at[k], self.recv_row.at[k], peer) for k, peer in enumerate(self.rows)
+        ]
+
+    def add_rows(self):
+        for copy in self.second:
+            copy.wait_recv()
+        if self.rows:
+            total = self.row_in[0]
+            for k in range(1, len(self.rows) + 1):
+                total = total + self.row_in[k]
+        else:
+            total = self.row_in[self.row]
+        self.spread[self.col] = total
+        mine = self.spread.at[self.col]
+        self.third = [
+            self.send(mine, mine, self.send_out.at[k], self.recv_out.at[k], peer) for k, peer in enumerate(self.cols)
+        ]
+
+    def end(self):
+        for copy in self.third:
+            copy.wait_recv()
+        self.out_ref[...] = self.spread[...]
+        for copy in self.first + self.second + self.third:
+            copy.wait_send()
+
+
+def sum_body(over_rows, row_total, col_total, part_ref, out_ref, extra_ref, *scratch):
+    gram = GramSum(over_rows, row_total, col_total, part_ref, out_ref, extra_ref, scratch)
+    greet(gram.cols + gram.rows)
+    gram.begin()
+    gram.add_cols()
+    gram.add_rows()
+    gram.end()
+
+
+def gram_shapes(gram, extra):
+    n = gram.shape[0]
     row_total, col_total = lax.axis_size("row"), lax.axis_size("col")
     piece = n // col_total
-    stacked = jnp.concatenate([part.reshape(col_total, piece, n), extra], axis=1)
-    dma = pltpu.SemaphoreType.DMA
-    total, rest = pl.pallas_call(
-        functools.partial(sum_body, over_rows, row_total, col_total),
-        in_specs=[pl.BlockSpec(memory_space=pltpu.VMEM)],
-        out_specs=(pl.BlockSpec(memory_space=pltpu.VMEM),) * 2,
-        out_shape=(
-            jax.ShapeDtypeStruct((col_total, piece, n), F32),
-            jax.ShapeDtypeStruct((extra.shape[1], n), F32),
-        ),
-        scratch_shapes=[
-            pltpu.VMEM((col_total - 1, piece + extra.shape[1], n), F32),
-            pltpu.VMEM((row_total, piece, n), F32),
-            pltpu.VMEM((col_total, piece, n), F32),
-            dma((col_total - 1,)), dma((col_total - 1,)),
-            dma((row_total - 1,)), dma((row_total - 1,)),
-            dma((col_total - 1,)), dma((col_total - 1,)),
-        ],
-        compiler_params=pltpu.CompilerParams(
-            vmem_limit_bytes=48 * 1024 * 1024, collective_id=call_id, has_side_effects=True
-        ),
+    stacked = jnp.concatenate([gram.reshape(col_total, piece, n), extra], axis=1)
+    shapes = (jax.ShapeDtypeStruct((col_total, piece, n), F32), jax.ShapeDtypeStruct((8, n), F32))
+    return stacked, shapes, gram_scratch(row_total, col_total, piece, n)
+
+
+def remote_params(call_id):
+    return pltpu.CompilerParams(vmem_limit_bytes=48 * 1024 * 1024, collective_id=call_id, has_side_effects=True)
+
+
+def in_vmem(count):
+    return (pl.BlockSpec(memory_space=pltpu.VMEM),) * count
+
+
+def sum_everywhere(gram, extra, call_id, name):
+    n = gram.shape[0]
+    stacked, shapes, scratch = gram_shapes(gram, extra)
+    total, _ = pl.pallas_call(
+        functools.partial(sum_body, True, lax.axis_size("row"), lax.axis_size("col")),
+        in_specs=in_vmem(1),
+        out_specs=in_vmem(2),
+        out_shape=shapes,
+        scratch_shapes=scratch,
+        compiler_params=remote_params(call_id),
         name=name,
         cost_estimate=pl.CostEstimate(flops=n * n * 10, bytes_accessed=40 * n * n, transcendentals=0),
     )(stacked)
-    return total.reshape(n, n), rest
+    return total.reshape(n, n)
 
 
 def chip_peers(col_total):
@@ -379,9 +430,11 @@
     return row, col, core, chip, chips, sibling, ahead
 
 
-def reduce_body(col_total, terms_ref, out_ref, from_core, joined, from_chip, send_core, recv_core, send_chip, recv_chip):
+def reduce_body(row_total, col_total, terms_ref, part_ref, out_ref, total_ref, extra_ref, from_core, joined, from_chip, send_core, recv_core, send_chip, recv_chip, *scratch):
     row, col, core, chip, chips, sibling, ahead = chip_peers(col_total)
-    greet([sibling] + ahead)
+    gram = GramSum(False, row_total, col_total, part_ref, total_ref, extra_ref, scratch)
+    greet(gram.cols)
+    gram.begin()
     order = list(range(1, chips)) + [0]
     near, far = {}, {}
     for k in order:
@@ -401,45 +454,53 @@
         )
         copy.start()
         far[k] = copy
+    gram.add_cols()
+    gram.add_rows()
     near[0].wait_recv()
     total = terms_ref[col] + from_core[0]
     for k in order[:-1]:
         far[k].wait_recv()
         total = total + from_chip[k - 1]
     out_ref[...] = total
+    gram.end()
     for copy in list(near.values()) + list(far.values()):
         copy.wait_send()
 
 
-def reduce_over_col(terms, call_id):
+def reduce_over_col(terms, gram, extra, call_id):
     rows, rank = terms.shape
     col_total = lax.axis_size("col")
     chips = col_total // 2
     piece = rows // col_total
     dma = pltpu.SemaphoreType.DMA
-    return pl.pallas_call(
-        functools.partial(reduce_body, col_total),
-        in_specs=[pl.BlockSpec(memory_space=pltpu.VMEM)],
-        out_specs=pl.BlockSpec(memory_space=pltpu.VMEM),
-        out_shape=jax.ShapeDtypeStruct((piece, rank), F32),
+    stacked, shapes, scratch = gram_shapes(gram, extra)
+    left, total, rest = pl.pallas_call(
+        functools.partial(reduce_body, lax.axis_size("row"), col_total),
+        in_specs=in_vmem(2),
+        out_specs=in_vmem(3),
+        out_shape=(jax.ShapeDtypeStruct((piece, rank), F32),) + shapes,
         scratch_shapes=[
             pltpu.VMEM((chips, piece, rank), F32),
             pltpu.VMEM((chips - 1, piece, rank), F32),
             pltpu.VMEM((chips - 1, piece, rank), F32),
             dma((chips,)), dma((chips,)), dma((chips - 1,)), dma((chips - 1,)),
-        ],
-        compiler_params=pltpu.CompilerParams(
-            vmem_limit_bytes=48 * 1024 * 1024, collective_id=call_id, has_side_effects=True
-        ),
+        ] + scratch,
+        compiler_params=remote_params(call_id),
         name="left_reduce",
         cost_estimate=pl.CostEstimate(flops=rows * rank, bytes_accessed=40 * rows * rank, transcendentals=0),
-    )(terms.reshape(col_total, piece, rank))
-
-
-def gather_body(col_total, piece_ref, out_ref, held, send_core, recv_core, send_chip, recv_chip):
+    )(terms.reshape(col_total, piece, rank), stacked)
+    return left, total.reshape(gram.shape), rest
+
+
+def gather_body(
+    row_total, col_total, piece_ref, part_ref, out_ref, total_ref, extra_ref,
+    held, send_core, recv_core, send_chip, recv_chip, *scratch,
+):
     row, col, core, chip, chips, sibling, ahead = chip_peers(col_total)
+    gram = GramSum(True, row_total, col_total, part_ref, total_ref, extra_ref, scratch)
     held[col] = piece_ref[...]
-    greet([sibling] + ahead)
+    greet(gram.cols + gram.rows)
+    gram.begin()
 
     def send(slot, target, send_sem, recv_sem):
         copy = pltpu.make_async_remote_copy(
@@ -451,38 +512,41 @@
 
     far = [send(col, ahead[k - 1], send_chip.at[k - 1], recv_chip.at[k - 1]) for k in range(1, chips)]
     near = [send(col, sibling, send_core.at[0], recv_core.at[0])]
+    gram.add_cols()
     for k in range(1, chips):
+        if k == chips - 1:
+            gram.add_rows()
         far[k - 1].wait_recv()
         source = 2 * ring_place(chip, chips - k, chips) + core
         near.append(send(source, sibling, send_core.at[k], recv_core.at[k]))
     for copy in near:
         copy.wait_recv()
     out_ref[...] = held[...]
+    gram.end()
     for copy in near + far:
         copy.wait_send()
 
 
-def gather_over_col(piece, call_id):
+def gather_over_col(piece, gram, extra, call_id):
     rows, width = piece.shape
     col_total = lax.axis_size("col")
     chips = col_total // 2
     dma = pltpu.SemaphoreType.DMA
-    whole = pl.pallas_call(
-        functools.partial(gather_body, col_total),
-        in_specs=[pl.BlockSpec(memory_space=pltpu.VMEM)],
-        out_specs=pl.BlockSpec(memory_space=pltpu.VMEM),
-        out_shape=jax.ShapeDtypeStruct((col_total, rows, width), piece.dtype),
+    stacked, shapes, scratch = gram_shapes(gram, extra)
+    whole, total, _ = pl.pallas_call(
+        functools.partial(gather_body, lax.axis_size("row"), col_total),
+        in_specs=in_vmem(2),
+        out_specs=in_vmem(3),
+        out_shape=(jax.ShapeDtypeStruct((col_total, rows, width), piece.dtype),) + shapes,
         scratch_shapes=[
             pltpu.VMEM((col_total, rows, width), piece.dtype),
             dma((chips,)), dma((chips,)), dma((chips - 1,)), dma((chips - 1,)),
-        ],
-        compiler_params=pltpu.CompilerParams(
-            vmem_limit_bytes=48 * 1024 * 1024, collective_id=call_id, has_side_effects=True
-        ),
+        ] + scratch,
+        compiler_params=remote_params(call_id),
         name="left_gather",
         cost_estimate=pl.CostEstimate(flops=rows, bytes_accessed=80 * rows * width, transcendentals=0),
-    )(piece)
-    return whole.reshape(col_total * rows, width)
+    )(piece, stacked)
+    return whole.reshape(col_total * rows, width), total.reshape(gram.shape)
 
 
 def own_columns(unit, cols):
@@ -517,12 +581,6 @@
     flags = jnp.pad(flags[:, None, :], ((0, 0), (0, 7), (0, rank - cells)))
     blank = jnp.zeros((col_total, 8, rank), F32)
 
-    left_terms = left_sum(warm_start, factor_init)
-    gram_right = lax.dot_general(factor_init, factor_init, (((0,), (0,)), ((), ())), precision=EXACT)
-    gram_right, listed = sum_everywhere(gram_right, flags, False, 1, "start_gram")
-    present = (listed[0, :cells] > 0.5).astype(jnp.int32)
-    left_terms = reduce_over_col(left_terms, 2)
-
     wide = descriptors.astype(F32)
     unit = (
         wide * lax.rsqrt(descriptors.shape[1] * (jnp.mean(wide * wide, axis=1, keepdims=True) + EPSILON))
@@ -531,17 +589,25 @@
     row_count = lax.dynamic_slice_in_dim(image_counts, row_place * img_row, img_row, 0)
     col_count = lax.dynamic_slice_in_dim(image_counts, col_place * img_col, img_col, 0)
 
+    left_terms = left_sum(warm_start, factor_init)
+    gram_right = lax.dot_general(factor_init, factor_init, (((0,), (0,)), ((), ())), precision=EXACT)
+    left_terms, gram_right, col_unit = lax.optimization_barrier((left_terms, gram_right, col_unit))
+    left_terms, gram_right, listed = reduce_over_col(left_terms, gram_right, flags, 1)
+    present = (listed[0, :cells] > 0.5).astype(jnp.int32)
+
     left_pair, gram_left = left_apply(left_terms, ridge_inverse(gram_right))
-    left_pair = gather_over_col(left_pair, 3)
+    left_pair, gram_left = gather_over_col(left_pair, gram_left, blank, 2)
     right_terms = right_sum(left_pair, warm_start)
-    gram_left, right_terms = lax.optimization_barrier((gram_left, right_terms))
+    gram_late, right_terms, col_unit = lax.optimization_barrier((gram_left, right_terms, col_unit))
     right_terms = lax.psum_scatter(right_terms, "row", scatter_dimension=1, tiled=True)
-    gram_left = sum_everywhere(gram_left, blank, True, 4, "left_gram")[0]
-    right_pair, gram_right = right_apply(right_terms, ridge_inverse(gram_left))
+    half_match = half_matches(present, row_count, col_count, unit, col_unit)
+    inverse = ridge_inverse(gram_late)
+    right_terms, inverse, half_match = lax.optimization_barrier((right_terms, inverse, half_match))
+    right_pair, gram_right = right_apply(right_terms, inverse)
     right_pair = lax.all_gather(right_pair, "row", axis=1, tiled=True)
-    gram_right = sum_everywhere(gram_right, blank, True, 5, "right_gram")[0]
+    gram_right = sum_everywhere(gram_right, blank, 3, "right_gram")
     mix = second_mix(gram_right, gram_left)
-    return finish(present, row_count, col_count, unit, col_unit, left_pair, right_pair, mix)
+    return finish(half_match, left_pair, right_pair, mix)
 
 
 def solution(mesh):

time: 221 us -> 181 us (0.82)
  Pallas kernels: 160 us -> 132 us
  waiting for transfers between devices: 22.9 us -> 15.9 us
    ppermute x3, waiting for transfers between devices: 22.8 us -> 3.32 us  [own_columns(): found = found + lax.ppermute(held, ('row', 'col'), pairs)]
    pallas_call x6 -> x5, Pallas kernels: 105 us -> 88.1 us  [the longest x1 26.2 us: gather_over_col(): pl.pallas_call(functools.partial(gather_body, lax.axis_size('row'), col_t...]
    reduce_scatter x1, waiting for transfers between devices: 0.02 us -> 12.5 us  [local(): lax.psum_scatter(right_terms, 'row', scatter_dimension=1, tiled=True)]
    pallas_call x1, Pallas kernels: 21.2 us -> 15.4 us  [second_mix(): pl.pallas_call(second_body, out_shape=jax.ShapeDtypeStruct((n, n), F32),...]
    pallas_call x2, Pallas kernels: 18.2 us -> 13 us  [ridge_inverse(): pl.pallas_call(inverse_body, out_shape=jax.ShapeDtypeStruct(gram.shape, F...]
  transfers between devices with their start and end apart: 5 -> 5, of which waited for: 3 -> 2; matrix products, arithmetic and copies ran while one was open for 1% -> 2% of each run, Pallas kernels for 33% -> 31%
where the time goes in v3:
time: 181 us; the launch traced here: 180 us
  Pallas kernels  132 us (73%)
  waiting for transfers between devices  15.9 us (9%)
  between operations  14.3 us (8%)
  starting transfers between devices  8.65 us (5%)
  other arithmetic  3.96 us (2%)
  local copies, waits for them, and re-layouts  3.62 us (2%)
  matrix products  1.84 us (1%)
    pallas_call x1, Pallas kernels, gather_over_col(): pl.pallas_call(functools.partial(gather_body, lax.axis_size('row'), col_t...  26.2 us
    pallas_call x1, Pallas kernels, reduce_over_col(): pl.pallas_call(functools.partial(reduce_body, lax.axis_size('row'), col_t...  20.8 us
    pallas_call x1, Pallas kernels, sum_everywhere(): pl.pallas_call(functools.partial(sum_body, True, lax.axis_size('row'), la...  20.5 us
    pallas_call x1, Pallas kernels, second_mix(): pl.pallas_call(second_body, out_shape=jax.ShapeDtypeStruct((n, n), F32),...  15.4 us
    pallas_call x1, Pallas kernels, finish(): pl.pallas_call(functools.partial(finish_body, cols // KP), grid=(rows //...  13.8 us
    pallas_call x2, Pallas kernels, ridge_inverse(): pl.pallas_call(inverse_body, out_shape=jax.ShapeDtypeStruct(gram.shape, F...  13 us
    reduce_scatter x1, waiting for transfers between devices, local(): lax.psum_scatter(right_terms, 'row', scatter_dimension=1, tiled=True)  12.5 us
    ppermute x3, starting transfers between devices, own_columns(): found = found + lax.ppermute(held, ('row', 'col'), pairs)  8.57 us
  transfers between devices with their start and end apart: 5, of which 2 were waited for; matrix products, arithmetic and copies ran while one was open for 2% of the time, Pallas kernels for 31%

profile of v3, /device:TPU:0, one launch (start us, length us, event | category | flops | bytes accessed | tf_op | source)
XLA Modules:
  0.0 179.9 jit_solution(12039730101626666441)
XLA Ops:
  7.2 1.4 fusion
  8.6 1.4 fusion.1.row_unit_ref
  10.0 6.0 %collective-permute-start.1 = (bf16[1024,128]{1,0:T(8,128)(2,1)S(1)}, bf16[1024,128]{1,0:T(8,128)(2,1)S(1)}, u32[]{:S(2)}, u32[]{:S(2)}) collective-permute-start(bf16[1024,128]{1,0:T(8,128)(2,1)S(1)} %constant_dynamic-slice_fusion), channel_id=1, source_target_pairs={{0,16},{1,17},{10,26},{11,27},{20,4},{21,5},{30,14},{31,15}} | collective-permute-start | bytes 786440 | tf_op jit(solution)/shard_map/ppermute | solution.py:563
  16.0 1.3 collective-permute-start
  17.3 1.3 collective-permute-start.2
  18.7 0.8 fusion.3
  19.7 1.2 copy-done
  20.9 6.7 %left_sum.1 = f32[2048,256]{1,0:T(8,128)S(1)} custom-call(bf16[2048,1024]{1,0:T(8,128)(2,1)} %warm_ref.3, f32[1024,256]{1,0:T(8,128)S(1)} %copy-done), custom_call_target="tpu_custom_call" | custom-call | flops 2147483648 | bytes 4194304 | tf_op jit(solution)/shard_map/left_sum/pallas_call | solution.py:119
  27.6 1.8 %fusion.4 = f32[256,256]{1,0:T(8,128)S(1)} fusion(f32[1024,256]{1,0:T(8,128)S(1)} %copy-done), kind=kOutput, calls=%fused_computation.20 | convolution fusion | flops 805306368 | bytes 1310720 | tf_op jit(solution)/shard_map/dot_general | solution.py:593
  29.5 3.3 %collective-permute-done.2 = bf16[1024,128]{1,0:T(8,128)(2,1)S(1)} collective-permute-done((bf16[1024,128]{1,0:T(8,128)(2,1)S(1)}, bf16[1024,128]{1,0:T(8,128)(2,1)S(1)}, u32[]{:S(2)}, u32[]{:S(2)}) %collective-permute-start.2) | collective-permute-done | bytes 262176 | tf_op jit(solution)/shard_map/ppermute | solution.py:563
  33.0 20.8 %left_reduce.1 = (f32[256,256]{1,0:T(8,128)S(1)}, f32[8,32,256]{2,1,0:T(8,128)S(1)}, f32[8,256]{1,0:T(8,128)S(1)}) custom-call(f32[8,256,256]{2,1,0:T(8,128)S(1)} %bitcast.17, f32[8,40,256]{2,1,0:T(8,128)S(1)} %pad_maximum_fusion.part_ref), custom_call_target="tpu_custom_call" | custom-call | flops 524288 | bytes 20971520 | tf_op jit(solution)/shard_map/left_reduce/pallas_call | solution.py:477
  53.8 5.7 %ridge_inverse.2.inverse_ref = f32[256,256]{1,0:T(8,128)S(1)} custom-call(f32[256,256]{1,0:T(8,128)S(1)} %bitcast.24), custom_call_target="tpu_custom_call" | custom-call | flops 3355443200 | bytes 524288 | tf_op jit(solution)/shard_map/ridge_inverse/pallas_call | solution.py:75
  59.6 1.1 left_apply.1
  60.7 26.2 %left_gather.1 = (bf16[8,256,512]{2,1,0:T(8,128)(2,1)S(1)}, f32[8,32,256]{2,1,0:T(8,128)S(1)}, f32[8,256]{1,0:T(8,128)}) custom-call(bf16[256,512]{1,0:T(8,128)(2,1)S(1)} %get-tuple-element.25.piece_ref, f32[8,40,256]{2,1,0:T(8,128)S(1)} %concatenate.10.part_ref), custom_call_target="tpu_custom_call" | custom-call | flops 256 | bytes 10485760 | tf_op jit(solution)/shard_map/left_gather/pallas_call | solution.py:536
  86.9 6.1 %right_sum.1 = f32[256,1024]{1,0:T(8,128)} custom-call(bf16[2048,512]{1,0:T(8,128)(2,1)S(1)} %bitcast.20, bf16[2048,1024]{1,0:T(8,128)(2,1)} %warm_ref.3), custom_call_target="tpu_custom_call" | custom-call | flops 2147483648 | bytes 4194304 | tf_op jit(solution)/shard_map/right_sum/pallas_call | solution.py:148
  93.3 6.7 %half_matches.1.match_ref = f32[2048,1024]{1,0:T(8,128)} custom-call(s32[32]{0:T(128)S(1)} %fusion.2.present_ref, s32[8]{0:T(128)S(1)} %dynamic_slice.10.row_count_ref, s32[4]{0:T(128)S(1)} %dynamic_slice.11.col_count_ref, bf16[2048,128]{1,0:T(8,128)(2,1)S(1)} %fusion.1.row_unit_ref, bf16[1024,128]{1,0:T(8,128)(2,1)S(1)} %add_add_fusion.col_unit_ref), custom_call_target="tpu_custom_call" | custom-call | flops 536870912 | bytes 8388608 | tf_op jit(solution)/shard_map/half_matches/pallas_call | solution.py:231
  100.0 7.3 %ridge_inverse.3.inverse_ref = f32[256,256]{1,0:T(8,128)S(1)} custom-call(f32[256,256]{1,0:T(8,128)S(1)} %bitcast.22), custom_call_target="tpu_custom_call" | custom-call | flops 3355443200 | bytes 524288 | tf_op jit(solution)/shard_map/ridge_inverse/pallas_call | solution.py:75
  107.3 12.5 %reduce-scatter.2.cloned.1.call-done.terms_ref = f32[256,256]{1,0:T(8,128)} async-done(((f32[256,1024]{1,0:T(8,128)}), f32[256,256]{1,0:T(8,128)}) %reduce-scatter.2.cloned.1.call-update) | async-done | bytes 262160 | tf_op jit(solution)/shard_map/reduce_scatter | solution.py:602
  119.8 0.9 copy-done.1
  120.8 1.3 right_apply.1
  122.1 20.5 %right_gram.1 = (f32[8,32,256]{2,1,0:T(8,128)S(1)}, f32[8,256]{1,0:T(8,128)}) custom-call(f32[8,40,256]{2,1,0:T(8,128)S(1)} %concatenate.11.part_ref), custom_call_target="tpu_custom_call" | custom-call | flops 655360 | bytes 2621440 | tf_op jit(solution)/shard_map/right_gram/pallas_call | solution.py:410
  142.6 15.4 %second_mix.1.mix_ref = f32[256,256]{1,0:T(8,128)S(1)} custom-call(f32[256,256]{1,0:T(8,128)S(1)} %bitcast.25, f32[256,256]{1,0:T(8,128)S(1)} %bitcast.23), custom_call_target="tpu_custom_call" | custom-call | flops 6710886400 | bytes 786432 | tf_op jit(solution)/shard_map/second_mix/pallas_call | solution.py:98
  158.1 1.2 copy-done.2
  159.3 13.8 %finish.1 = (bf16[2048,1024]{1,0:T(8,128)(2,1)}, f32[2048,1024]{1,0:T(8,128)}) custom-call(f32[2048,1024]{1,0:T(8,128)} %half_matches.1.match_ref, bf16[2048,512]{1,0:T(8,128)(2,1)S(1)} %bitcast.21, bf16[512,1024]{1,0:T(8,128)(2,1)S(1)} %copy-done.2, f32[256,256]{1,0:T(8,128)S(1)} %second_mix.1.mix_ref), custom_call_target="tpu_custom_call" | custom-call | flops 6442450944 | bytes 20971520 | tf_op jit(solution)/shard_map/finish/pallas_call | solution.py:276
  (26 shorter events, 0.8 us)
Async XLA Ops:
  7.2 112.7 %reduce-scatter.2.cloned.1.call-start = ((), (), s32[]{:S(2)}) async-start(), calls=%async_computation.1 | async-start | bytes 1310720 | tf_op jit(solution)/shard_map/reduce_scatter | solution.py:602
  10.0 19.4 %collective-permute-start.1 = (bf16[1024,128]{1,0:T(8,128)(2,1)S(1)}, bf16[1024,128]{1,0:T(8,128)(2,1)S(1)}, u32[]{:S(2)}, u32[]{:S(2)}) collective-permute-start(bf16[1024,128]{1,0:T(8,128)(2,1)S(1)} %constant_dynamic-slice_fusion), channel_id=1, source_target_pairs={{0,16},{1,17},{10,26},{11,27},{20,4},{21,5},{30,14},{31,15}} | collective-permute-start | bytes 786440 | tf_op jit(solution)/shard_map/ppermute | solution.py:563
  16.0 13.4 %collective-permute-start = (bf16[1024,128]{1,0:T(8,128)(2,1)S(1)}, bf16[1024,128]{1,0:T(8,128)(2,1)S(1)}, u32[]{:S(2)}, u32[]{:S(2)}) collective-permute-start(bf16[1024,128]{1,0:T(8,128)(2,1)S(1)} %constant_dynamic-slice_fusion), channel_id=1, source_target_pairs={{0,8},{1,9},{10,18},{11,19},{20,28},{21,29},{30,6},{31,7}} | collective-permute-start | bytes 786440 | tf_op jit(solution)/shard_map/ppermute | solution.py:563
  17.3 15.5 %collective-permute-start.2 = (bf16[1024,128]{1,0:T(8,128)(2,1)S(1)}, bf16[1024,128]{1,0:T(8,128)(2,1)S(1)}, u32[]{:S(2)}, u32[]{:S(2)}) collective-permute-start(bf16[1024,128]{1,0:T(8,128)(2,1)S(1)} %constant_dynamic-slice_fusion), channel_id=1, source_target_pairs={{0,24},{1,25},{10,2},{11,3},{20,12},{21,13},{30,22},{31,23}} | collective-permute-start | bytes 786440 | tf_op jit(solution)/shard_map/ppermute | solution.py:563
  19.7 1.2 copy-start
  86.9 6.2 %copy-start.3 = (s32[32]{0:T(128)S(1)}, s32[32]{0:T(128)}, u32[]{:S(2)}) copy-start(s32[32]{0:T(128)} %param.6) | copy-start | bytes 388
  93.1 64.9 %all-gather.2.cloned.1.call-start = ((), (), s32[]{:S(2)}) async-start(), calls=%async_computation.2 | async-start | bytes 1310720 | tf_op jit(solution)/shard_map/all_gather | solution.py:607
  119.8 0.9 copy-start.1
  158.0 1.2 copy-start.2
Sparse Core Ops, SparseCore 0:
  93.2 26.5 reduce-scatter.1
  122.2 29.5 all-gather.1

commit v4 on v3

--- a/solution.py
+++ b/solution.py
@@ -132,12 +132,14 @@
     )(warm, right)
 
 
-def right_sum_body(left_ref, warm_ref, out_ref, turned_ref):
+def right_sum_body(left_ref, warm_ref, out_ref, gram_ref, turned_ref):
     rank = out_ref.shape[0]
 
     @pl.when(pl.program_id(0) == 0)
     def _():
         turned_ref[...] = left_ref[...].T
+        gram = dot32(turned_ref[...], left_ref[...])
+        gram_ref[...] = (gram[:rank, :rank] + gram[rank:, rank:]) + (gram[:rank, rank:] + gram[rank:, :rank])
 
     out_ref[...] = dot32(turned_ref[:rank, :], warm_ref[...]) + dot32(turned_ref[rank:, :], warm_ref[...])
 
@@ -152,8 +154,8 @@
             pl.BlockSpec((rows, 2 * rank), lambda i: (0, 0)),
             pl.BlockSpec((rows, KP), lambda i: (0, i)),
         ],
-        out_specs=pl.BlockSpec((rank, KP), lambda i: (0, i)),
-        out_shape=jax.ShapeDtypeStruct((rank, cols), F32),
+        out_specs=(pl.BlockSpec((rank, KP), lambda i: (0, i)), pl.BlockSpec((rank, rank), lambda i: (0, 0))),
+        out_shape=(jax.ShapeDtypeStruct((rank, cols), F32), jax.ShapeDtypeStruct((rank, rank), F32)),
         scratch_shapes=[pltpu.VMEM((2 * rank, rows), BF16)],
         compiler_params=PARAMS,
         name="right_sum",
@@ -161,20 +163,19 @@
     )(left_pair, warm)
 
 
-def left_apply_body(terms_ref, inverse_ref, pair_ref, gram_ref):
+def left_apply_body(terms_ref, inverse_ref, pair_ref):
     rank = terms_ref.shape[1]
     left = exact(terms_ref[...], inverse_ref[...])
     high, low = halves(left)
     pair_ref[:, :rank] = high
     pair_ref[:, rank:] = low
-    gram_ref[...] = exact(left.T, left)
 
 
 def left_apply(terms, inverse):
     rows, rank = terms.shape
     return pl.pallas_call(
         left_apply_body,
-        out_shape=(jax.ShapeDtypeStruct((rows, 2 * rank), BF16), jax.ShapeDtypeStruct((rank, rank), F32)),
+        out_shape=jax.ShapeDtypeStruct((rows, 2 * rank), BF16),
         compiler_params=PARAMS,
         name="left_apply",
     )(terms, inverse)
@@ -318,10 +319,11 @@
 
 
 class GramSum:
-    def __init__(self, over_rows, row_total, col_total, part_ref, out_ref, extra_ref, scratch):
+    def __init__(self, over_cols, over_rows, row_total, col_total, part_ref, out_ref, extra_ref, scratch):
         self.part_ref, self.out_ref, self.extra_ref = part_ref, out_ref, extra_ref
         (self.col_in, self.row_in, self.spread, self.send_col, self.recv_col,
          self.send_row, self.recv_row, self.send_out, self.recv_out) = scratch
+        self.over_cols = over_cols
         self.row, self.col = lax.axis_index("row"), lax.axis_index("col")
         self.cols = [(self.row, ring_place(self.col, k, col_total)) for k in range(1, col_total)]
         self.rows = (
@@ -339,7 +341,7 @@
     def begin(self):
         self.first = [
             self.send(self.part_ref.at[peer[1]], self.col_in.at[k], self.send_col.at[k], self.recv_col.at[k], peer)
-            for k, peer in enumerate(self.cols)
+            for k, peer in enumerate(self.cols if self.over_cols else [])
         ]
 
     def add_cols(self):
@@ -378,8 +380,8 @@
             copy.wait_send()
 
 
-def sum_body(over_rows, row_total, col_total, part_ref, out_ref, extra_ref, *scratch):
-    gram = GramSum(over_rows, row_total, col_total, part_ref, out_ref, extra_ref, scratch)
+def sum_body(over_cols, row_total, col_total, part_ref, out_ref, extra_ref, *scratch):
+    gram = GramSum(over_cols, True, row_total, col_total, part_ref, out_ref, extra_ref, scratch)
     greet(gram.cols + gram.rows)
     gram.begin()
     gram.add_cols()
@@ -404,11 +406,11 @@
     return (pl.BlockSpec(memory_space=pltpu.VMEM),) * count
 
 
-def sum_everywhere(gram, extra, call_id, name):
+def sum_everywhere(gram, extra, over_cols, call_id, name):
     n = gram.shape[0]
     stacked, shapes, scratch = gram_shapes(gram, extra)
     total, _ = pl.pallas_call(
-        functools.partial(sum_body, True, lax.axis_size("row"), lax.axis_size("col")),
+        functools.partial(sum_body, over_cols, lax.axis_size("row"), lax.axis_size("col")),
         in_specs=in_vmem(1),
         out_specs=in_vmem(2),
         out_shape=shapes,
@@ -432,7 +434,7 @@
 
 def reduce_body(row_total, col_total, terms_ref, part_ref, out_ref, total_ref, extra_ref, from_core, joined, from_chip, send_core, recv_core, send_chip, recv_chip, *scratch):
     row, col, core, chip, chips, sibling, ahead = chip_peers(col_total)
-    gram = GramSum(False, row_total, col_total, part_ref, total_ref, extra_ref, scratch)
+    gram = GramSum(True, False, row_total, col_total, part_ref, total_ref, extra_ref, scratch)
     greet(gram.cols)
     gram.begin()
     order = list(range(1, chips)) + [0]
@@ -493,14 +495,11 @@
 
 
 def gather_body(
-    row_total, col_total, piece_ref, part_ref, out_ref, total_ref, extra_ref,
-    held, send_core, recv_core, send_chip, recv_chip, *scratch,
+    col_total, piece_ref, out_ref, held, send_core, recv_core, send_chip, recv_chip
 ):
     row, col, core, chip, chips, sibling, ahead = chip_peers(col_total)
-    gram = GramSum(True, row_total, col_total, part_ref, total_ref, extra_ref, scratch)
     held[col] = piece_ref[...]
-    greet(gram.cols + gram.rows)
-    gram.begin()
+    greet([sibling] + ahead)
 
     def send(slot, target, send_sem, recv_sem):
         copy = pltpu.make_async_remote_copy(
@@ -512,41 +511,36 @@
 
     far = [send(col, ahead[k - 1], send_chip.at[k - 1], recv_chip.at[k - 1]) for k in range(1, chips)]
     near = [send(col, sibling, send_core.at[0], recv_core.at[0])]
-    gram.add_cols()
     for k in range(1, chips):
-        if k == chips - 1:
-            gram.add_rows()
         far[k - 1].wait_recv()
         source = 2 * ring_place(chip, chips - k, chips) + core
         near.append(send(source, sibling, send_core.at[k], recv_core.at[k]))
     for copy in near:
         copy.wait_recv()
     out_ref[...] = held[...]
-    gram.end()
     for copy in near + far:
         copy.wait_send()
 
 
-def gather_over_col(piece, gram, extra, call_id):
+def gather_over_col(piece, call_id):
     rows, width = piece.shape
     col_total = lax.axis_size("col")
     chips = col_total // 2
     dma = pltpu.SemaphoreType.DMA
-    stacked, shapes, scratch = gram_shapes(gram, extra)
-    whole, total, _ = pl.pallas_call(
-        functools.partial(gather_body, lax.axis_size("row"), col_total),
-        in_specs=in_vmem(2),
-        out_specs=in_vmem(3),
-        out_shape=(jax.ShapeDtypeStruct((col_total, rows, width), piece.dtype),) + shapes,
+    whole = pl.pallas_call(
+        functools.partial(gather_body, col_total),
+        in_specs=in_vmem(1),
+        out_specs=pl.BlockSpec(memory_space=pltpu.VMEM),
+        out_shape=jax.ShapeDtypeStruct((col_total, rows, width), piece.dtype),
         scratch_shapes=[
             pltpu.VMEM((col_total, rows, width), piece.dtype),
             dma((chips,)), dma((chips,)), dma((chips - 1,)), dma((chips - 1,)),
-        ] + scratch,
+        ],
         compiler_params=remote_params(call_id),
         name="left_gather",
         cost_estimate=pl.CostEstimate(flops=rows, bytes_accessed=80 * rows * width, transcendentals=0),
-    )(piece, stacked)
-    return whole.reshape(col_total * rows, width), total.reshape(gram.shape)
+    )(piece)
+    return whole.reshape(col_total * rows, width)
 
 
 def own_columns(unit, cols):
@@ -595,17 +589,17 @@
     left_terms, gram_right, listed = reduce_over_col(left_terms, gram_right, flags, 1)
     present = (listed[0, :cells] > 0.5).astype(jnp.int32)
 
-    left_pair, gram_left = left_apply(left_terms, ridge_inverse(gram_right))
-    left_pair, gram_left = gather_over_col(left_pair, gram_left, blank, 2)
-    right_terms = right_sum(left_pair, warm_start)
-    gram_late, right_terms, col_unit = lax.optimization_barrier((gram_left, right_terms, col_unit))
+    left_pair = gather_over_col(left_apply(left_terms, ridge_inverse(gram_right)), 2)
+    right_terms, gram_left = right_sum(left_pair, warm_start)
+    gram_left, right_terms, col_unit = lax.optimization_barrier((gram_left, right_terms, col_unit))
     right_terms = lax.psum_scatter(right_terms, "row", scatter_dimension=1, tiled=True)
     half_match = half_matches(present, row_count, col_count, unit, col_unit)
-    inverse = ridge_inverse(gram_late)
+    gram_left = sum_everywhere(gram_left, blank, False, 4, "left_gram")
+    inverse = ridge_inverse(gram_left)
     right_terms, inverse, half_match = lax.optimization_barrier((right_terms, inverse, half_match))
     right_pair, gram_right = right_apply(right_terms, inverse)
     right_pair = lax.all_gather(right_pair, "row", axis=1, tiled=True)
-    gram_right = sum_everywhere(gram_right, blank, 3, "right_gram")
+    gram_right = sum_everywhere(gram_right, blank, True, 3, "right_gram")
     mix = second_mix(gram_right, gram_left)
     return finish(half_match, left_pair, right_pair, mix)
 

time: 181 us -> 173 us (0.956)
  waiting for transfers between devices: 15.9 us -> 3.67 us
  Pallas kernels: 132 us -> 134 us
    reduce_scatter x1, waiting for transfers between devices: 12.5 us -> 0.24 us  [local(): lax.psum_scatter(right_terms, 'row', scatter_dimension=1, tiled=True)]
    pallas_call x3 -> x4, Pallas kernels: 47.8 us -> 49.1 us  [the longest x2 32.2 us: sum_everywhere(): pl.pallas_call(functools.partial(sum_body, over_cols, lax.axis_size('row'...]
    unnamed x8 -> x10, local copies, waits for them, and re-layouts: 3.39 us -> 4.36 us
  transfers between devices with their start and end apart: 5 -> 5, of which waited for: 2 -> 3; matrix products, arithmetic and copies ran while one was open for 2% -> 2% of each run, Pallas kernels for 31% -> 40%
where the time goes in v4:
time: 173 us; the launch traced here: 171 us
  Pallas kernels  134 us (77%)
  between operations  14.3 us (8%)
  starting transfers between devices  8.65 us (5%)
  local copies, waits for them, and re-layouts  4.59 us (3%)
  other arithmetic  3.96 us (2%)
  waiting for transfers between devices  3.67 us (2%)
  matrix products  1.84 us (1%)
    pallas_call x2, Pallas kernels, sum_everywhere(): pl.pallas_call(functools.partial(sum_body, over_cols, lax.axis_size('row'...  32.2 us
    pallas_call x1, Pallas kernels, reduce_over_col(): pl.pallas_call(functools.partial(reduce_body, lax.axis_size('row'), col_t...  20.8 us
    pallas_call x1, Pallas kernels, gather_over_col(): pl.pallas_call(functools.partial(gather_body, col_total), in_specs=in_vme...  16.6 us
    pallas_call x1, Pallas kernels, second_mix(): pl.pallas_call(second_body, out_shape=jax.ShapeDtypeStruct((n, n), F32),...  15.4 us
    pallas_call x2, Pallas kernels, ridge_inverse(): pl.pallas_call(inverse_body, out_shape=jax.ShapeDtypeStruct(gram.shape, F...  14.1 us
    pallas_call x1, Pallas kernels, finish(): pl.pallas_call(functools.partial(finish_body, cols // KP), grid=(rows //...  13.8 us
    ppermute x3, starting transfers between devices, own_columns(): found = found + lax.ppermute(held, ('row', 'col'), pairs)  8.57 us
    pallas_call x1, Pallas kernels, left_sum(): pl.pallas_call(left_sum_body, grid=(rows // KP,), in_specs=[pl.BlockSpec(...  6.67 us
  transfers between devices with their start and end apart: 5, of which 3 were waited for; matrix products, arithmetic and copies ran while one was open for 2% of the time, Pallas kernels for 40%

profile of v4, /device:TPU:0, one launch (start us, length us, event | category | flops | bytes accessed | tf_op | source)
XLA Modules:
  0.0 170.8 jit_solution(17082578851838410873)
XLA Ops:
  7.2 1.4 fusion
  8.6 1.4 fusion.1.row_unit_ref
  10.0 6.0 %collective-permute-start.1 = (bf16[1024,128]{1,0:T(8,128)(2,1)S(1)}, bf16[1024,128]{1,0:T(8,128)(2,1)S(1)}, u32[]{:S(2)}, u32[]{:S(2)}) collective-permute-start(bf16[1024,128]{1,0:T(8,128)(2,1)S(1)} %constant_dynamic-slice_fusion), channel_id=1, source_target_pairs={{0,16},{1,17},{10,26},{11,27},{20,4},{21,5},{30,14},{31,15}} | collective-permute-start | bytes 786440 | tf_op jit(solution)/shard_map/ppermute | solution.py:557
  16.0 1.3 collective-permute-start
  17.3 1.3 collective-permute-start.2
  18.7 0.8 fusion.3
  19.7 1.2 copy-done
  20.9 6.7 %left_sum.1 = f32[2048,256]{1,0:T(8,128)S(1)} custom-call(bf16[2048,1024]{1,0:T(8,128)(2,1)} %warm_ref.3, f32[1024,256]{1,0:T(8,128)S(1)} %copy-done), custom_call_target="tpu_custom_call" | custom-call | flops 2147483648 | bytes 4194304 | tf_op jit(solution)/shard_map/left_sum/pallas_call | solution.py:119
  27.6 1.8 %fusion.4 = f32[256,256]{1,0:T(8,128)S(1)} fusion(f32[1024,256]{1,0:T(8,128)S(1)} %copy-done), kind=kOutput, calls=%fused_computation.20 | convolution fusion | flops 805306368 | bytes 1310720 | tf_op jit(solution)/shard_map/dot_general | solution.py:587
  29.5 3.3 %collective-permute-done.2 = bf16[1024,128]{1,0:T(8,128)(2,1)S(1)} collective-permute-done((bf16[1024,128]{1,0:T(8,128)(2,1)S(1)}, bf16[1024,128]{1,0:T(8,128)(2,1)S(1)}, u32[]{:S(2)}, u32[]{:S(2)}) %collective-permute-start.2) | collective-permute-done | bytes 262176 | tf_op jit(solution)/shard_map/ppermute | solution.py:557
  33.0 20.8 %left_reduce.1 = (f32[256,256]{1,0:T(8,128)S(1)}, f32[8,32,256]{2,1,0:T(8,128)S(1)}, f32[8,256]{1,0:T(8,128)S(1)}) custom-call(f32[8,256,256]{2,1,0:T(8,128)S(1)} %bitcast.19, f32[8,40,256]{2,1,0:T(8,128)S(1)} %pad_maximum_fusion.part_ref), custom_call_target="tpu_custom_call" | custom-call | flops 524288 | bytes 20971520 | tf_op jit(solution)/shard_map/left_reduce/pallas_call | solution.py:479
  53.8 6.8 %ridge_inverse.2.inverse_ref = f32[256,256]{1,0:T(8,128)S(1)} custom-call(f32[256,256]{1,0:T(8,128)S(1)} %bitcast.24), custom_call_target="tpu_custom_call" | custom-call | flops 3355443200 | bytes 524288 | tf_op jit(solution)/shard_map/ridge_inverse/pallas_call | solution.py:75
  61.1 16.6 %left_gather.1 = bf16[8,256,512]{2,1,0:T(8,128)(2,1)S(1)} custom-call(bf16[256,512]{1,0:T(8,128)(2,1)S(1)} %left_apply.1.piece_ref), custom_call_target="tpu_custom_call" | custom-call | flops 256 | bytes 10485760 | tf_op jit(solution)/shard_map/left_gather/pallas_call | solution.py:530
  77.6 6.0 %right_sum.1 = (f32[256,1024]{1,0:T(8,128)S(1)}, f32[256,256]{1,0:T(8,128)S(1)}) custom-call(bf16[2048,512]{1,0:T(8,128)(2,1)S(1)} %bitcast.17, bf16[2048,1024]{1,0:T(8,128)(2,1)} %warm_ref.3), custom_call_target="tpu_custom_call" | custom-call | flops 2147483648 | bytes 4194304 | tf_op jit(solution)/shard_map/right_sum/pallas_call | solution.py:150
  83.7 1.0 copy-done.1
  84.9 13.7 %left_gram.1 = (f32[8,32,256]{2,1,0:T(8,128)S(1)}, f32[8,256]{1,0:T(8,128)}) custom-call(f32[8,40,256]{2,1,0:T(8,128)S(1)} %concatenate.10.part_ref), custom_call_target="tpu_custom_call" | custom-call | flops 655360 | bytes 2621440 | tf_op jit(solution)/shard_map/left_gram/pallas_call | solution.py:412
  98.6 6.6 %half_matches.1.match_ref = f32[2048,1024]{1,0:T(8,128)} custom-call(s32[32]{0:T(128)S(1)} %fusion.2.present_ref, s32[8]{0:T(128)S(1)} %dynamic_slice.10.row_count_ref, s32[4]{0:T(128)S(1)} %dynamic_slice.11.col_count_ref, bf16[2048,128]{1,0:T(8,128)(2,1)S(1)} %fusion.1.row_unit_ref, bf16[1024,128]{1,0:T(8,128)(2,1)S(1)} %add_add_fusion.col_unit_ref), custom_call_target="tpu_custom_call" | custom-call | flops 536870912 | bytes 8388608 | tf_op jit(solution)/shard_map/half_matches/pallas_call | solution.py:232
  105.2 7.3 %ridge_inverse.3.inverse_ref = f32[256,256]{1,0:T(8,128)S(1)} custom-call(f32[256,256]{1,0:T(8,128)S(1)} %bitcast.22), custom_call_target="tpu_custom_call" | custom-call | flops 3355443200 | bytes 524288 | tf_op jit(solution)/shard_map/ridge_inverse/pallas_call | solution.py:75
  112.7 0.9 copy-done.2
  113.7 1.3 right_apply.1
  115.0 18.5 %right_gram.1 = (f32[8,32,256]{2,1,0:T(8,128)S(1)}, f32[8,256]{1,0:T(8,128)}) custom-call(f32[8,40,256]{2,1,0:T(8,128)S(1)} %concatenate.11.part_ref), custom_call_target="tpu_custom_call" | custom-call | flops 655360 | bytes 2621440 | tf_op jit(solution)/shard_map/right_gram/pallas_call | solution.py:412
  133.5 15.4 %second_mix.1.mix_ref = f32[256,256]{1,0:T(8,128)S(1)} custom-call(f32[256,256]{1,0:T(8,128)S(1)} %bitcast.25, f32[256,256]{1,0:T(8,128)S(1)} %bitcast.23), custom_call_target="tpu_custom_call" | custom-call | flops 6710886400 | bytes 786432 | tf_op jit(solution)/shard_map/second_mix/pallas_call | solution.py:98
  149.0 1.2 copy-done.3
  150.2 13.8 %finish.1 = (bf16[2048,1024]{1,0:T(8,128)(2,1)}, f32[2048,1024]{1,0:T(8,128)}) custom-call(f32[2048,1024]{1,0:T(8,128)} %half_matches.1.match_ref, bf16[2048,512]{1,0:T(8,128)(2,1)S(1)} %bitcast.18, bf16[512,1024]{1,0:T(8,128)(2,1)S(1)} %copy-done.3, f32[256,256]{1,0:T(8,128)S(1)} %second_mix.1.mix_ref), custom_call_target="tpu_custom_call" | custom-call | flops 6442450944 | bytes 20971520 | tf_op jit(solution)/shard_map/finish/pallas_call | solution.py:277
  (29 shorter events, 1.5 us)
Async XLA Ops:
  7.2 105.6 %reduce-scatter.2.cloned.1.call-start = ((), (), s32[]{:S(2)}) async-start(), calls=%async_computation.1 | async-start | bytes 1310720 | tf_op jit(solution)/shard_map/reduce_scatter | solution.py:595
  10.0 19.4 %collective-permute-start.1 = (bf16[1024,128]{1,0:T(8,128)(2,1)S(1)}, bf16[1024,128]{1,0:T(8,128)(2,1)S(1)}, u32[]{:S(2)}, u32[]{:S(2)}) collective-permute-start(bf16[1024,128]{1,0:T(8,128)(2,1)S(1)} %constant_dynamic-slice_fusion), channel_id=1, source_target_pairs={{0,16},{1,17},{10,26},{11,27},{20,4},{21,5},{30,14},{31,15}} | collective-permute-start | bytes 786440 | tf_op jit(solution)/shard_map/ppermute | solution.py:557
  16.0 13.4 %collective-permute-start = (bf16[1024,128]{1,0:T(8,128)(2,1)S(1)}, bf16[1024,128]{1,0:T(8,128)(2,1)S(1)}, u32[]{:S(2)}, u32[]{:S(2)}) collective-permute-start(bf16[1024,128]{1,0:T(8,128)(2,1)S(1)} %constant_dynamic-slice_fusion), channel_id=1, source_target_pairs={{0,8},{1,9},{10,18},{11,19},{20,28},{21,29},{30,6},{31,7}} | collective-permute-start | bytes 786440 | tf_op jit(solution)/shard_map/ppermute | solution.py:557
  17.3 15.5 %collective-permute-start.2 = (bf16[1024,128]{1,0:T(8,128)(2,1)S(1)}, bf16[1024,128]{1,0:T(8,128)(2,1)S(1)}, u32[]{:S(2)}, u32[]{:S(2)}) collective-permute-start(bf16[1024,128]{1,0:T(8,128)(2,1)S(1)} %constant_dynamic-slice_fusion), channel_id=1, source_target_pairs={{0,24},{1,25},{10,2},{11,3},{20,12},{21,13},{30,22},{31,23}} | collective-permute-start | bytes 786440 | tf_op jit(solution)/shard_map/ppermute | solution.py:557
  19.7 1.2 copy-start
  77.6 7.1 %copy-start.4 = (s32[32]{0:T(128)S(1)}, s32[32]{0:T(128)}, u32[]{:S(2)}) copy-start(s32[32]{0:T(128)} %param.6) | copy-start | bytes 388
  83.6 1.0 copy-start.1
  84.6 64.3 %all-gather.2.cloned.1.call-start = ((), (), s32[]{:S(2)}) async-start(), calls=%async_computation.2 | async-start | bytes 1310720 | tf_op jit(solution)/shard_map/all_gather | solution.py:601
  112.7 0.9 copy-start.2
  149.0 1.2 copy-start.3
Sparse Core Ops, SparseCore 0:
  84.8 27.9 reduce-scatter.1
  115.1 33.8 all-gather.1
